TPU v7x, 512 devices: a whole 4x4x16 slice. The times are simulated.
512 devices in a mesh: dp: 4 (over x), tm: 8 (over y, core), rows: 16 (over z).
Axes of the slice: x: 4, y: 4, z: 16, core: 2. Of those that a mesh axis runs over, the one named last changes fastest.
Arguments:
- clips: bfloat16 [4, 16, 64, 64, 256], P('dp', 'tm', 'rows'), may hold values from -6 to 6
- segment_ids: int32 [4, 16], P('dp'), may hold values from 0 to 3, never falling along the last dimension, each value on 1 to 8 neighbouring positions
- spatial_weight: bfloat16 [2, 9, 256, 256], replicated, may hold values from -0.125 to 0.125
- temporal_weight: bfloat16 [2, 3, 256, 256], replicated, may hold values from -0.21875 to 0.21875
- upstream: bfloat16 [4, 16, 64, 64, 256], P('dp', 'tm', 'rows'), may hold values from -6 to 6
Outputs:
- input_grad: bfloat16 [4, 16, 64, 64, 256], P('dp', 'tm', 'rows')
- features: bfloat16 [4, 16, 64, 64, 256], P('dp', 'tm', 'rows')
- temporal_grad: float32 [1536, 256], P('rows')
Inputs may be any that keep to these rules, and one draw needn't show every extreme that they name: `segment_ids`: frame numbers of packed clips in each row never fall; each packed clip has 1 to 8 frames and one has exactly 8.
All inputs are finite; a program needn't handle non-finite values.
Results may differ from a plain program's by a relative error of at most 0.015.
Values may be sent and summed in bfloat16 or wider, within the bound.
A program may use at most 64 MiB of HBM per device.

v0:
```python
import jax
import jax.numpy as jnp
from jax import lax
from jax.sharding import PartitionSpec as P


def with_halo(cells, sides, width):
    for axis, dim in sides:
        count = lax.axis_size(axis)
        ends = count - 1
        head = lax.slice_in_dim(cells, 0, width, axis=dim)
        tail = lax.slice_in_dim(cells, cells.shape[dim] - width, cells.shape[dim], axis=dim)
        cells = jnp.concatenate(
            [
                lax.ppermute(tail, axis, [(i, (i + 1) % count) for i in range(ends)]),
                cells,
                lax.ppermute(head, axis, [((i + 1) % count, i) for i in range(ends)]),
            ],
            axis=dim,
        )
    return cells


def from_behind(value, axis, steps):
    count = lax.axis_size(axis)
    first, last = (max(0, -steps), min(count, count - steps))
    return lax.ppermute(value, axis, [(source, source + steps) for source in range(first, last)])


def silu_slope(values):
    sigma = jax.nn.sigmoid(values)
    return sigma * (1.0 + values * (1.0 - sigma))


def frame_masks(segments, first_frame, frame_count):
    frame_total = segments.shape[0]
    positions = jnp.arange(frame_total, dtype=jnp.int32)
    global_pos = first_frame + jnp.arange(frame_count, dtype=jnp.int32)

    def lookup(frame_pos):
        matches = positions[None, :] == frame_pos[:, None]
        return jnp.sum(jnp.where(matches, segments[None, :], 0), axis=1)

    own_ids = lookup(global_pos)
    masks = []
    for offset in range(3):
        source = global_pos - offset
        masks.append((source >= 0) & (lookup(source) == own_ids))
    return masks


def spatial_local(padded, weights, flipped):
    height = padded.shape[2] - 2
    columns = padded.shape[3]
    channels = padded.shape[4]
    wide = jnp.pad(padded, ((0, 0), (0, 0), (0, 0), (1, 1), (0, 0)))
    out_shape = padded.shape[:2] + (height, columns, channels)
    accumulated = jnp.zeros(out_shape, jnp.float32)
    for tap_index in range(9):
        row_off = tap_index // 3
        col_off = tap_index % 3
        matrix = weights[tap_index]
        if flipped:
            row_off = 2 - row_off
            col_off = 2 - col_off
            matrix = matrix.T
        window = wide[:, :, row_off : row_off + height, col_off : col_off + columns, :]
        product = jnp.dot(window.reshape(-1, channels), matrix, preferred_element_type=jnp.float32)
        accumulated = accumulated + product.reshape(out_shape)
    return accumulated


def forward_layer(layer_in, space_weights, time_weights, own_masks):
    frames_dev = layer_in.shape[1]
    channels = layer_in.shape[4]
    padded = with_halo(layer_in, (("rows", 2),), 1)
    spatial_sum = spatial_local(padded, space_weights, False)
    activated = jax.nn.silu(spatial_sum).astype(jnp.bfloat16)
    prior = from_behind(activated, "tm", 1)
    joined = jnp.concatenate([prior, activated], axis=1)
    accumulated = jnp.zeros(activated.shape, jnp.float32)
    for offset in range(3):
        source = joined[:, frames_dev - offset : 2 * frames_dev - offset]
        product = jnp.dot(
            source.reshape(-1, channels), time_weights[offset], preferred_element_type=jnp.float32
        )
        accumulated = accumulated + jnp.where(
            own_masks[offset][None, :, None, None, None], product.reshape(activated.shape), 0.0
        )
    layer_out = (layer_in.astype(jnp.float32) + accumulated).astype(jnp.bfloat16)
    return (layer_out, spatial_sum, joined)


def backward_layer(
    grad_in, spatial_sum, joined, space_weights, time_weights, own_masks, next_masks
):
    frames_dev = grad_in.shape[1]
    channels = grad_in.shape[4]
    later = from_behind(grad_in, "tm", -1)
    extended = jnp.concatenate([grad_in, later], axis=1)
    grad_act = jnp.zeros(grad_in.shape, jnp.float32)
    pieces = []
    for offset in range(3):
        both_masks = jnp.concatenate([own_masks[offset], next_masks[offset]])
        masked = jnp.where(
            both_masks[None, :, None, None, None], extended, jnp.zeros_like(extended)
        )
        lifted = masked[:, offset : offset + frames_dev]
        product = jnp.dot(
            lifted.reshape(-1, channels), time_weights[offset].T, preferred_element_type=jnp.float32
        )
        grad_act = grad_act + product.reshape(grad_in.shape)
        source = joined[:, frames_dev - offset : 2 * frames_dev - offset].reshape(-1, channels)
        own_part = masked[:, :frames_dev].reshape(-1, channels)
        pieces.append(
            lax.dot_general(
                source, own_part, (((0,), (0,)), ((), ())), preferred_element_type=jnp.float32
            )
        )
    grad_pre = (grad_act * silu_slope(spatial_sum)).astype(jnp.bfloat16)
    padded = with_halo(grad_pre, (("rows", 2),), 1)
    back = spatial_local(padded, space_weights, True)
    grad_out = (grad_in.astype(jnp.float32) + back).astype(jnp.bfloat16)
    return (grad_out, jnp.stack(pieces))


def local(clips, segment_ids, spatial_weight, temporal_weight, upstream):
    frames_dev = clips.shape[1]
    segments = segment_ids[0]
    chain_pos = lax.axis_index("tm")
    own_masks = frame_masks(segments, chain_pos * frames_dev, frames_dev)
    next_masks = frame_masks(segments, (chain_pos + 1) * frames_dev, frames_dev)
    layer_count = spatial_weight.shape[0]
    layer_in = clips
    saved = []
    for layer_index in range(layer_count):
        layer_in, spatial_sum, joined = forward_layer(
            layer_in, spatial_weight[layer_index], temporal_weight[layer_index], own_masks
        )
        saved.append((spatial_sum, joined))
    grad_in = upstream
    layer_grads = [None] * layer_count
    for layer_index in reversed(range(layer_count)):
        spatial_sum, joined = saved[layer_index]
        grad_in, weight_grad = backward_layer(
            grad_in,
            spatial_sum,
            joined,
            spatial_weight[layer_index],
            temporal_weight[layer_index],
            own_masks,
            next_masks,
        )
        flat_grad = weight_grad.reshape(-1, weight_grad.shape[-1])
        layer_grads[layer_index] = flat_grad
    partial_grad = jnp.concatenate(layer_grads, axis=0)
    share = partial_grad.shape[0] // lax.axis_size("rows")
    combined = lax.psum(partial_grad, ("dp", "tm", "rows"))
    result = lax.dynamic_slice_in_dim(combined, lax.axis_index("rows") * share, share, 0)
    return (grad_in, layer_in, result)


def solution(mesh):
    return jax.shard_map(
        local,
        mesh=mesh,
        in_specs=(
            P("dp", "tm", "rows", None, None),
            P("dp", None),
            P(),
            P(),
            P("dp", "tm", "rows", None, None),
        ),
        out_specs=(
            P("dp", "tm", "rows", None, None),
            P("dp", "tm", "rows", None, None),
            P("rows", None),
        ),
        check_vma=False,
    )
```

profile of v0, /device:TPU:1, one launch (start us, length us, event | category | flops | bytes accessed | tf_op | source)
XLA Modules:
  0.0 562.2 jit_solution(16869984013026459328)
XLA Ops:
  7.2 1.7 fusion.208
  8.9 4.4 collective-permute-start.1
  13.3 1.3 collective-permute-start.2
  14.6 5.7 %collective-permute-start = (bf16[1,2,4,64,256]{4,3,2,1,0:T(8,128)(2,1)}, bf16[1,2,4,64,256]{4,3,2,1,0:T(8,128)(2,1)S(1)}, u32[]{:S(2)}, u32[]{:S(2)}) collective-permute-start(bf16[1,2,4,64,256]{4,3,2,1,0:T(8,128)(2,1)} %param.9), channel_id=1, source_target_pairs={{16,0},{32,16},{48,32},{64,48},{80,64},{96,80},{112,96},{17,1},{33... | collective-permute-start | bytes 786440 | tf_op jit(solution)/shard_map/ppermute | solution.py:27
  20.4 0.5 broadcast_add_fusion
  20.9 0.6 broadcast_add_fusion.2
  21.4 0.5 iota_add_fusion
  22.0 1.0 constant_dynamic-update-slice_fusion.1
  23.0 0.9 fusion.188
  24.2 1.1 fusion.34
  25.2 1.1 fusion.71
  28.1 0.3 multiply_convert_fusion.1
  28.4 1.9 collective-permute-start.3
  31.0 2.6 collective-permute-done.3
  34.1 4.3 collective-permute-start.4
  38.4 1.3 collective-permute-start.5
  39.7 0.3 convolution_add_fusion.31
  40.0 3.4 collective-permute-done.5
  45.5 0.3 multiply_convert_fusion
  46.0 0.3 fusion.22
  46.4 3.2 collective-permute-start.6
  49.6 1.3 collective-permute-start.7
  50.9 0.3 convolution_bitcast_fusion.2
  51.2 5.8 %collective-permute-start.11 = (bf16[1,2,4,64,256]{4,3,2,1,0:T(8,128)(2,1)S(1)}, bf16[1,2,4,64,256]{4,3,2,1,0:T(8,128)(2,1)S(1)}, u32[]{:S(2)}, u32[]{:S(2)}) collective-permute-start(bf16[1,2,4,64,256]{4,3,2,1,0:T(8,128)(2,1)S(1)} %bitcast.463), channel_id=1, source_target_pairs={{0,16},{16,32},{32,48},{48,64},{64,80},{80,96},{96,112},{1,17},{17... | collective-permute-start | bytes 786440 | tf_op jit(solution)/shard_map/ppermute | solution.py:27
  57.2 0.3 fusion.54
  57.7 0.3 convolution_add_fusion.15
  58.3 0.3 convolution_add_fusion.13
  59.1 0.3 convolution_add_fusion.10
  59.5 0.3 fusion.19
  59.8 1.9 collective-permute-start.8
  61.7 0.3 convolution_bitcast_fusion.1
  62.0 0.3 convolution_bitcast_fusion
  62.6 1.0 fusion.21
  63.5 6.0 %collective-permute-done.8 = bf16[1,2,4,64,256]{4,3,2,1,0:T(8,128)(2,1)S(1)} collective-permute-done((bf16[1,2,4,64,256]{4,3,2,1,0:T(8,128)(2,1)S(1)}, bf16[1,2,4,64,256]{4,3,2,1,0:T(8,128)(2,1)S(1)}, u32[]{:S(2)}, u32[]{:S(2)}) %collective-permute-start.8) | collective-permute-done | bytes 262176 | tf_op jit(solution)/shard_map/ppermute | solution.py:27
  69.5 0.3 fusion.110
  70.2 0.3 fusion.23
  70.6 4.9 collective-permute-start.9
  75.5 1.3 collective-permute-start.10
  76.8 0.3 convolution_bitcast_fusion.5
  77.1 0.3 convolution_bitcast_fusion.4
  77.7 1.2 pad_maximum_fusion
  79.0 1.8 collective-permute-done.10
  81.9 0.3 convolution_add_fusion.4
  82.5 0.3 convolution_add_fusion.2
  82.8 0.3 convolution_add_fusion.1
  83.0 1.0 fusion.18
  84.0 469.8 %all-reduce.6.cloned.1.call-done = f32[1536,256]{1,0:T(8,128)} async-done(((f32[1536,256]{1,0:T(8,128)}), f32[1536,256]{1,0:T(8,128)}) %all-reduce.6.cloned.1.call-update) | async-done | bytes 1572880 | tf_op jit(solution)/shard_map/psum | solution.py:158
  553.8 1.5 constant_dynamic-slice_fusion
  (70 shorter events, 9.0 us)
Async XLA Ops:
  7.2 19.5 %copy-start.1 = (bf16[1,2,4,64,256]{4,3,2,1,0:T(8,128)(2,1)S(1)}, bf16[1,2,4,64,256]{4,3,2,1,0:T(8,128)(2,1)}, u32[]{:S(2)}) copy-start(bf16[1,2,4,64,256]{4,3,2,1,0:T(8,128)(2,1)} %param.5) | copy-start | bytes 786436
  7.2 19.2 %copy-start = (bf16[2,9,256,256]{3,2,1,0:T(8,128)(2,1)S(1)}, bf16[2,9,256,256]{3,2,1,0:T(8,128)(2,1)}, u32[]{:S(2)}) copy-start(bf16[2,9,256,256]{3,2,1,0:T(8,128)(2,1)} %param.7) | copy-start | bytes 7077892
  7.2 546.6 %all-reduce.6.cloned.1.call-start = ((), (), s32[]{:S(2)}) async-start(), calls=%async_computation | async-start | bytes 3145728 | tf_op jit(solution)/shard_map/psum | solution.py:158
  8.9 15.2 %collective-permute-start.1 = (bf16[1,2,1,64,256]{4,3,2,1,0:T(8,128)(2,1)}, bf16[1,2,1,64,256]{4,3,2,1,0:T(8,128)(2,1)S(1)}, u32[]{:S(2)}, u32[]{:S(2)}) collective-permute-start(bf16[1,2,1,64,256]{4,3,2,1,0:T(8,128)(2,1)} %get-tuple-element.19), channel_id=1, source_target_pairs={{0,1},{1,2},{2,3},{3,4},{4,5},{5,6},{6,7},{7,8},{8,9},{9,10},{10,1... | collective-permute-start | bytes 196616 | tf_op jit(solution)/shard_map/ppermute | solution.py:15
  13.3 10.9 %collective-permute-start.2 = (bf16[1,2,1,64,256]{4,3,2,1,0:T(8,128)(2,1)}, bf16[1,2,1,64,256]{4,3,2,1,0:T(8,128)(2,1)S(1)}, u32[]{:S(2)}, u32[]{:S(2)}) collective-permute-start(bf16[1,2,1,64,256]{4,3,2,1,0:T(8,128)(2,1)} %get-tuple-element.20), channel_id=1, source_target_pairs={{1,0},{2,1},{3,2},{4,3},{5,4},{6,5},{7,6},{8,7},{9,8},{10,9},{11,1... | collective-permute-start | bytes 196616 | tf_op jit(solution)/shard_map/ppermute | solution.py:17
  14.6 16.0 %collective-permute-start = (bf16[1,2,4,64,256]{4,3,2,1,0:T(8,128)(2,1)}, bf16[1,2,4,64,256]{4,3,2,1,0:T(8,128)(2,1)S(1)}, u32[]{:S(2)}, u32[]{:S(2)}) collective-permute-start(bf16[1,2,4,64,256]{4,3,2,1,0:T(8,128)(2,1)} %param.9), channel_id=1, source_target_pairs={{16,0},{32,16},{48,32},{64,48},{80,64},{96,80},{112,96},{17,1},{33... | collective-permute-start | bytes 786440 | tf_op jit(solution)/shard_map/ppermute | solution.py:27
  27.8 2.5 copy-start.2
  28.4 5.2 collective-permute-start.3
  34.1 5.9 %collective-permute-start.4 = (bf16[1,2,1,64,256]{4,3,2,1,0:T(8,128)(2,1)S(1)}, bf16[1,2,1,64,256]{4,3,2,1,0:T(8,128)(2,1)S(1)}, u32[]{:S(2)}, u32[]{:S(2)}) collective-permute-start(bf16[1,2,1,64,256]{4,3,2,1,0:T(8,128)(2,1)S(1)} %get-tuple-element.17), channel_id=1, source_target_pairs={{0,1},{1,2},{2,3},{3,4},{4,5},{5,6},{6,7},{7,8},{8,9},{9,10},{10,1... | collective-permute-start | bytes 196616 | tf_op jit(solution)/shard_map/ppermute | solution.py:15
  38.4 5.0 collective-permute-start.5
  46.4 10.6 %collective-permute-start.6 = (bf16[1,2,1,64,256]{4,3,2,1,0:T(8,128)(2,1)S(1)}, bf16[1,2,1,64,256]{4,3,2,1,0:T(8,128)(2,1)S(1)}, u32[]{:S(2)}, u32[]{:S(2)}) collective-permute-start(bf16[1,2,1,64,256]{4,3,2,1,0:T(8,128)(2,1)S(1)} %get-tuple-element.15), channel_id=1, source_target_pairs={{0,1},{1,2},{2,3},{3,4},{4,5},{5,6},{6,7},{7,8},{8,9},{9,10},{10,1... | collective-permute-start | bytes 196616 | tf_op jit(solution)/shard_map/ppermute | solution.py:15
  49.6 7.4 %collective-permute-start.7 = (bf16[1,2,1,64,256]{4,3,2,1,0:T(8,128)(2,1)S(1)}, bf16[1,2,1,64,256]{4,3,2,1,0:T(8,128)(2,1)S(1)}, u32[]{:S(2)}, u32[]{:S(2)}) collective-permute-start(bf16[1,2,1,64,256]{4,3,2,1,0:T(8,128)(2,1)S(1)} %get-tuple-element.16), channel_id=1, source_target_pairs={{1,0},{2,1},{3,2},{4,3},{5,4},{6,5},{7,6},{8,7},{9,8},{10,9},{11,1... | collective-permute-start | bytes 196616 | tf_op jit(solution)/shard_map/ppermute | solution.py:17
  51.2 10.5 %collective-permute-start.11 = (bf16[1,2,4,64,256]{4,3,2,1,0:T(8,128)(2,1)S(1)}, bf16[1,2,4,64,256]{4,3,2,1,0:T(8,128)(2,1)S(1)}, u32[]{:S(2)}, u32[]{:S(2)}) collective-permute-start(bf16[1,2,4,64,256]{4,3,2,1,0:T(8,128)(2,1)S(1)} %bitcast.463), channel_id=1, source_target_pairs={{0,16},{16,32},{32,48},{48,64},{64,80},{80,96},{96,112},{1,17},{17... | collective-permute-start | bytes 786440 | tf_op jit(solution)/shard_map/ppermute | solution.py:27
  58.5 1.0 copy-start.3
  59.8 9.7 %collective-permute-start.8 = (bf16[1,2,4,64,256]{4,3,2,1,0:T(8,128)(2,1)S(1)}, bf16[1,2,4,64,256]{4,3,2,1,0:T(8,128)(2,1)S(1)}, u32[]{:S(2)}, u32[]{:S(2)}) collective-permute-start(bf16[1,2,4,64,256]{4,3,2,1,0:T(8,128)(2,1)S(1)} %fusion.19), channel_id=1, source_target_pairs={{16,0},{32,16},{48,32},{64,48},{80,64},{96,80},{112,96},{17,1},{33... | collective-permute-start | bytes 786440 | tf_op jit(solution)/shard_map/ppermute | solution.py:27
  70.6 8.4 %collective-permute-start.9 = (bf16[1,2,1,64,256]{4,3,2,1,0:T(8,128)(2,1)S(1)}, bf16[1,2,1,64,256]{4,3,2,1,0:T(8,128)(2,1)S(1)}, u32[]{:S(2)}, u32[]{:S(2)}) collective-permute-start(bf16[1,2,1,64,256]{4,3,2,1,0:T(8,128)(2,1)S(1)} %get-tuple-element.13), channel_id=1, source_target_pairs={{0,1},{1,2},{2,3},{3,4},{4,5},{5,6},{6,7},{7,8},{8,9},{9,10},{10,1... | collective-permute-start | bytes 196616 | tf_op jit(solution)/shard_map/ppermute | solution.py:15
  75.5 5.3 collective-permute-start.10
Sparse Core Ops, SparseCore 0:
  79.1 474.6 all-reduce.5
where the time goes:
time: 563 us; the launch traced here: 562 us
  waiting for transfers between devices  484 us (86%)
  starting transfers between devices  37.3 us (7%)
  matrix products  16.2 us (3%)
  between operations  14.7 us (3%)
  other arithmetic  5.94 us (1%)
    psum x1, waiting for transfers between devices, local(): combined = lax.psum(partial_grad, ('dp', 'tm', 'rows'))  470 us
    ppermute x4, starting transfers between devices, with_halo(): lax.ppermute(tail, axis, [(i, (i + 1) % count) for i in range(ends)])  16.7 us
    ppermute x4, starting transfers between devices, from_behind(): lax.ppermute(value, axis, [(source, source + steps) for source in range(f...  15.4 us
  transfers between devices with their start and end apart: 13, of which 5 were waited for; matrix products, arithmetic and copies ran while one was open for 3% of the time, Pallas kernels for 0%

commit v1 on v0

--- a/solution.py
+++ b/solution.py
@@ -1,6 +1,8 @@
 import jax
 import jax.numpy as jnp
 from jax import lax
+from jax.experimental import pallas as pl
+from jax.experimental.pallas import tpu as pltpu
 from jax.sharding import PartitionSpec as P
 
 
@@ -123,6 +125,150 @@
     grad_out = (grad_in.astype(jnp.float32) + back).astype(jnp.bfloat16)
     return (grad_out, jnp.stack(pieces))
 
+XS, YS, CORES, ZS = 4, 4, 2, 16
+CHIPS = XS * YS
+PLANE = CHIPS * CORES
+PIECE = 6
+HALF = 128
+
+
+def sum_kernel(part_ref, out_ref, arranged, send_pair, recv_pair, send_plane, recv_plane, send_z, recv_z,
+               total, recv_all, sems):
+    x = lax.axis_index("dp")
+    t = lax.axis_index("tm")
+    z = lax.axis_index("rows")
+    core = t % CORES
+    chip = x * YS + t // CORES
+    place = x * (YS * CORES) + t
+
+    def plane_id(other):
+        return {"dp": other // (YS * CORES), "tm": other % (YS * CORES)}
+
+    def chip_id(other):
+        return {"dp": other // YS, "tm": (other % YS) * CORES + core}
+
+    barrier = pltpu.get_barrier_semaphore()
+
+    @pl.loop(1, PLANE)
+    def _(step):
+        pl.semaphore_signal(barrier, inc=1, device_id=plane_id((place + step) % PLANE))
+
+    @pl.loop(1, ZS)
+    def _(step):
+        pl.semaphore_signal(barrier, inc=1, device_id={"rows": (z + step) % ZS})
+
+    @pl.loop(0, XS)
+    def _(high):
+        for block in range(ZS):
+            rows = part_ref[pl.ds(pl.multiple_of(96 * block + PIECE * YS * high, 8), PIECE * YS), :]
+            for low in range(YS):
+                arranged[high * YS + low, PIECE * block : PIECE * (block + 1), :] = rows[
+                    PIECE * low : PIECE * (low + 1)
+                ]
+
+    @pl.loop(0, CHIPS)
+    def _(group):
+        rows = arranged[group]
+        other = jnp.where(core == 0, rows[:, HALF:], rows[:, :HALF])
+        send_pair[group] = other.astype(jnp.bfloat16)
+
+    pl.semaphore_wait(barrier, PLANE - 1 + ZS - 1)
+    pair = pltpu.make_async_remote_copy(
+        src_ref=send_pair, dst_ref=recv_pair, send_sem=sems.at[0], recv_sem=sems.at[1],
+        device_id={"tm": t + 1 - 2 * core},
+    )
+    pair.start()
+    pair.wait()
+
+    @pl.loop(0, CHIPS)
+    def _(group):
+        rows = arranged[group]
+        own = jnp.where(core == 0, rows[:, :HALF], rows[:, HALF:])
+        send_plane[group] = (own + recv_pair[group].astype(jnp.float32)).astype(jnp.bfloat16)
+
+    @pl.loop(1, CHIPS)
+    def _(step):
+        other = (chip + step) % CHIPS
+        pltpu.make_async_remote_copy(
+            src_ref=send_plane.at[other], dst_ref=recv_plane.at[chip], send_sem=sems.at[2], recv_sem=sems.at[3],
+            device_id=chip_id(other),
+        ).start()
+
+    recv_plane[chip] = send_plane[chip]
+    both = pltpu.make_async_remote_copy(
+        src_ref=send_plane.at[pl.ds(0, CHIPS - 1)], dst_ref=recv_plane.at[pl.ds(0, CHIPS - 1)],
+        send_sem=sems.at[2], recv_sem=sems.at[3], device_id=chip_id((chip + 1) % CHIPS),
+    )
+    both.wait()
+    summed = recv_plane[0].astype(jnp.float32)
+    for group in range(1, CHIPS):
+        summed = summed + recv_plane[group].astype(jnp.float32)
+    for block in range(ZS):
+        send_z[block, :PIECE, :] = summed[PIECE * block : PIECE * (block + 1), :]
+        send_z[block, PIECE:, :] = jnp.zeros((8 - PIECE, HALF), jnp.float32)
+
+    @pl.loop(1, ZS)
+    def _(step):
+        other = (z + step) % ZS
+        pltpu.make_async_remote_copy(
+            src_ref=send_z.at[other], dst_ref=recv_z.at[z], send_sem=sems.at[4], recv_sem=sems.at[5],
+            device_id={"rows": other},
+        ).start()
+
+    recv_z[z] = send_z[z]
+    pltpu.make_async_remote_copy(
+        src_ref=send_z.at[pl.ds(0, ZS - 1)], dst_ref=recv_z.at[pl.ds(0, ZS - 1)],
+        send_sem=sems.at[4], recv_sem=sems.at[5], device_id={"rows": (z + 1) % ZS},
+    ).wait()
+    final = recv_z[0]
+    for block in range(1, ZS):
+        final = final + recv_z[block]
+    total[...] = final
+
+    @pl.loop(1, PLANE)
+    def _(step):
+        pltpu.make_async_remote_copy(
+            src_ref=total, dst_ref=recv_all.at[place], send_sem=sems.at[6], recv_sem=sems.at[7],
+            device_id=plane_id((place + step) % PLANE),
+        ).start()
+
+    recv_all[place] = final
+    pltpu.make_async_remote_copy(
+        src_ref=recv_all.at[pl.ds(0, PLANE - 1)], dst_ref=recv_all.at[pl.ds(0, PLANE - 1)],
+        send_sem=sems.at[6], recv_sem=sems.at[7], device_id=plane_id((place + 1) % PLANE),
+    ).wait()
+    for group in range(CHIPS):
+        for half in range(CORES):
+            out_ref[PIECE * group : PIECE * (group + 1), HALF * half : HALF * (half + 1)] = recv_all[
+                group * CORES + half, :PIECE, :
+            ]
+
+
+def summed_gradient(partial_grad):
+    rows, columns = partial_grad.shape
+    deep = PIECE * ZS
+    return pl.pallas_call(
+        sum_kernel,
+        out_shape=jax.ShapeDtypeStruct((rows // ZS, columns), jnp.float32),
+        in_specs=[pl.BlockSpec(memory_space=pltpu.VMEM)],
+        out_specs=pl.BlockSpec(memory_space=pltpu.VMEM),
+        scratch_shapes=[
+            pltpu.VMEM((CHIPS, deep, columns), jnp.float32),
+            pltpu.VMEM((CHIPS, deep, HALF), jnp.bfloat16),
+            pltpu.VMEM((CHIPS, deep, HALF), jnp.bfloat16),
+            pltpu.VMEM((CHIPS, deep, HALF), jnp.bfloat16),
+            pltpu.VMEM((CHIPS, deep, HALF), jnp.bfloat16),
+            pltpu.VMEM((ZS, 8, HALF), jnp.float32),
+            pltpu.VMEM((ZS, 8, HALF), jnp.float32),
+            pltpu.VMEM((8, HALF), jnp.float32),
+            pltpu.VMEM((PLANE, 8, HALF), jnp.float32),
+            pltpu.SemaphoreType.DMA((8,)),
+        ],
+        compiler_params=pltpu.CompilerParams(
+            collective_id=0, has_side_effects=True, vmem_limit_bytes=40 * 1024 * 1024
+        ),
+    )(partial_grad)
+
 
 def local(clips, segment_ids, spatial_weight, temporal_weight, upstream):
     frames_dev = clips.shape[1]
@@ -154,9 +300,7 @@
         flat_grad = weight_grad.reshape(-1, weight_grad.shape[-1])
         layer_grads[layer_index] = flat_grad
     partial_grad = jnp.concatenate(layer_grads, axis=0)
-    share = partial_grad.shape[0] // lax.axis_size("rows")
-    combined = lax.psum(partial_grad, ("dp", "tm", "rows"))
-    result = lax.dynamic_slice_in_dim(combined, lax.axis_index("rows") * share, share, 0)
+    result = summed_gradient(partial_grad)
     return (grad_in, layer_in, result)
 
 

time: 563 us -> 110 us (0.20)
  waiting for transfers between devices: 484 us -> 10.9 us
  Pallas kernels: 0 us -> 36.9 us
  between operations: 14.7 us -> 1.36 us
    psum x1 -> x0, waiting for transfers between devices: 470 us -> none  [local(): combined = lax.psum(partial_grad, ('dp', 'tm', 'rows'))]
    pallas_call x0 -> x1, Pallas kernels: none -> 36.9 us  [summed_gradient(): pl.pallas_call(sum_kernel, out_shape=jax.ShapeDtypeStruct((rows // ZS, co...]
  transfers between devices with their start and end apart: 13 -> 12, of which waited for: 5 -> 3; matrix products, arithmetic and copies ran while one was open for 3% -> 12% of each run, Pallas kernels for 0% -> 34%
where the time goes in v1:
time: 110 us
  starting transfers between devices  38.4 us (35%)
  Pallas kernels  36.9 us (34%)
  matrix products  16.2 us (15%)
  waiting for transfers between devices  10.9 us (10%)
  other arithmetic  3.15 us (3%)
  local copies, waits for them, and re-layouts  2.86 us (3%)
  between operations  1.36 us (1%)
    pallas_call x1, Pallas kernels, summed_gradient(): pl.pallas_call(sum_kernel, out_shape=jax.ShapeDtypeStruct((rows // ZS, co...  36.9 us
    ppermute x4, starting transfers between devices, with_halo(): lax.ppermute(tail, axis, [(i, (i + 1) % count) for i in range(ends)])  17.9 us
    ppermute x4, starting transfers between devices, from_behind(): lax.ppermute(value, axis, [(source, source + steps) for source in range(f...  15.4 us
    dot_general x36, matrix products, spatial_local(): jnp.dot(window.reshape(-1, channels), matrix, preferred_element_type=jnp....  10.7 us
    ppermute x4, waiting for transfers between devices, from_behind(): lax.ppermute(value, axis, [(source, source + steps) for source in range(f...  7.45 us
    ppermute x4, starting transfers between devices, with_halo(): lax.ppermute(head, axis, [((i + 1) % count, i) for i in range(ends)])  5.17 us
    ppermute x4, waiting for transfers between devices, with_halo(): lax.ppermute(head, axis, [((i + 1) % count, i) for i in range(ends)])  3.43 us
  transfers between devices with their start and end apart: 12, of which 3 were waited for; matrix products, arithmetic and copies ran while one was open for 12% of the time, Pallas kernels for 34%

profile of v1, /device:TPU:1, one launch (start us, length us, event | category | flops | bytes accessed | tf_op | source)
XLA Modules:
  0.0 109.8 jit_solution(17186951825279626679)
XLA Ops:
  0.7 1.0 fusion.208
  1.7 4.4 %collective-permute-start.1 = (bf16[1,2,1,64,256]{4,3,2,1,0:T(8,128)(2,1)S(1)}, bf16[1,2,1,64,256]{4,3,2,1,0:T(8,128)(2,1)S(1)}, u32[]{:S(2)}, u32[]{:S(2)}) collective-permute-start(bf16[1,2,1,64,256]{4,3,2,1,0:T(8,128)(2,1)S(1)} %get-tuple-element.19), channel_id=1, source_target_pairs={{0,1},{1,2},{2,3},{3,4},{4,5},{5,6},{6,7},{7,8},{8,9},{9,10},{10,1... | collective-permute-start | bytes 196616 | tf_op jit(solution)/shard_map/ppermute | solution.py:17
  6.1 1.3 %collective-permute-start.2 = (bf16[1,2,1,64,256]{4,3,2,1,0:T(8,128)(2,1)S(1)}, bf16[1,2,1,64,256]{4,3,2,1,0:T(8,128)(2,1)S(1)}, u32[]{:S(2)}, u32[]{:S(2)}) collective-permute-start(bf16[1,2,1,64,256]{4,3,2,1,0:T(8,128)(2,1)S(1)} %get-tuple-element.20), channel_id=1, source_target_pairs={{1,0},{2,1},{3,2},{4,3},{5,4},{6,5},{7,6},{8,7},{9,8},{10,9},{11,1... | collective-permute-start | bytes 196616 | tf_op jit(solution)/shard_map/ppermute | solution.py:19
  7.4 5.7 %collective-permute-start = (bf16[1,2,4,64,256]{4,3,2,1,0:T(8,128)(2,1)}, bf16[1,2,4,64,256]{4,3,2,1,0:T(8,128)(2,1)S(1)}, u32[]{:S(2)}, u32[]{:S(2)}) collective-permute-start(bf16[1,2,4,64,256]{4,3,2,1,0:T(8,128)(2,1)} %param.9), channel_id=1, source_target_pairs={{16,0},{32,16},{48,32},{64,48},{80,64},{96,80},{112,96},{17,1},{33... | collective-permute-start | bytes 786440 | tf_op jit(solution)/shard_map/ppermute | solution.py:29
  13.2 1.0 constant_dynamic-update-slice_fusion.1
  14.2 0.9 fusion.188
  15.3 1.1 fusion.34
  16.4 1.1 %fusion.71 = f32[2,4,64,256]{3,2,1,0:T(8,128)S(1)} fusion(bf16[1,2,6,66,256]{4,3,2,1,0:T(8,128)(2,1)S(1)} %fusion.34, bf16[2,9,256,256]{3,2,1,0:T(8,128)(2,1)} %param.7), kind=kOutput, calls=%fused_computation.167 | convolution fusion | flops 67108864 | bytes 917504 | tf_op jit(solution)/shard_map/dot_general | solution.py:70
  19.2 0.3 multiply_convert_fusion.1
  19.6 1.9 %collective-permute-start.3 = (bf16[1,2,4,64,256]{4,3,2,1,0:T(8,128)(2,1)S(1)}, bf16[1,2,4,64,256]{4,3,2,1,0:T(8,128)(2,1)S(1)}, u32[]{:S(2)}, u32[]{:S(2)}) collective-permute-start(bf16[1,2,4,64,256]{4,3,2,1,0:T(8,128)(2,1)S(1)} %bitcast.460), channel_id=1, source_target_pairs={{0,16},{16,32},{32,48},{48,64},{64,80},{80,96},{96,112},{1,17},{17... | collective-permute-start | bytes 786440 | tf_op jit(solution)/shard_map/ppermute | solution.py:29
  22.2 2.6 %collective-permute-done.3 = bf16[1,2,4,64,256]{4,3,2,1,0:T(8,128)(2,1)S(1)} collective-permute-done((bf16[1,2,4,64,256]{4,3,2,1,0:T(8,128)(2,1)S(1)}, bf16[1,2,4,64,256]{4,3,2,1,0:T(8,128)(2,1)S(1)}, u32[]{:S(2)}, u32[]{:S(2)}) %collective-permute-start.3) | collective-permute-done | bytes 262176 | tf_op jit(solution)/shard_map/ppermute | solution.py:29
  25.3 4.3 %collective-permute-start.4 = (bf16[1,2,1,64,256]{4,3,2,1,0:T(8,128)(2,1)S(1)}, bf16[1,2,1,64,256]{4,3,2,1,0:T(8,128)(2,1)S(1)}, u32[]{:S(2)}, u32[]{:S(2)}) collective-permute-start(bf16[1,2,1,64,256]{4,3,2,1,0:T(8,128)(2,1)S(1)} %get-tuple-element.17), channel_id=1, source_target_pairs={{0,1},{1,2},{2,3},{3,4},{4,5},{5,6},{6,7},{7,8},{8,9},{9,10},{10,1... | collective-permute-start | bytes 196616 | tf_op jit(solution)/shard_map/ppermute | solution.py:17
  29.6 1.3 %collective-permute-start.5 = (bf16[1,2,1,64,256]{4,3,2,1,0:T(8,128)(2,1)S(1)}, bf16[1,2,1,64,256]{4,3,2,1,0:T(8,128)(2,1)S(1)}, u32[]{:S(2)}, u32[]{:S(2)}) collective-permute-start(bf16[1,2,1,64,256]{4,3,2,1,0:T(8,128)(2,1)S(1)} %get-tuple-element.18), channel_id=1, source_target_pairs={{1,0},{2,1},{3,2},{4,3},{5,4},{6,5},{7,6},{8,7},{9,8},{10,9},{11,1... | collective-permute-start | bytes 196616 | tf_op jit(solution)/shard_map/ppermute | solution.py:19
  30.9 0.3 convolution_add_fusion.31
  31.1 3.4 %collective-permute-done.5 = bf16[1,2,1,64,256]{4,3,2,1,0:T(8,128)(2,1)S(1)} collective-permute-done((bf16[1,2,1,64,256]{4,3,2,1,0:T(8,128)(2,1)S(1)}, bf16[1,2,1,64,256]{4,3,2,1,0:T(8,128)(2,1)S(1)}, u32[]{:S(2)}, u32[]{:S(2)}) %collective-permute-start.5) | collective-permute-done | bytes 65568 | tf_op jit(solution)/shard_map/ppermute | solution.py:19
  36.6 0.3 multiply_convert_fusion
  37.1 0.3 fusion.22
  37.5 4.5 %collective-permute-start.6 = (bf16[1,2,1,64,256]{4,3,2,1,0:T(8,128)(2,1)S(1)}, bf16[1,2,1,64,256]{4,3,2,1,0:T(8,128)(2,1)S(1)}, u32[]{:S(2)}, u32[]{:S(2)}) collective-permute-start(bf16[1,2,1,64,256]{4,3,2,1,0:T(8,128)(2,1)S(1)} %get-tuple-element.15), channel_id=1, source_target_pairs={{0,1},{1,2},{2,3},{3,4},{4,5},{5,6},{6,7},{7,8},{8,9},{9,10},{10,1... | collective-permute-start | bytes 196616 | tf_op jit(solution)/shard_map/ppermute | solution.py:17
  42.0 1.3 %collective-permute-start.7 = (bf16[1,2,1,64,256]{4,3,2,1,0:T(8,128)(2,1)S(1)}, bf16[1,2,1,64,256]{4,3,2,1,0:T(8,128)(2,1)S(1)}, u32[]{:S(2)}, u32[]{:S(2)}) collective-permute-start(bf16[1,2,1,64,256]{4,3,2,1,0:T(8,128)(2,1)S(1)} %get-tuple-element.16), channel_id=1, source_target_pairs={{1,0},{2,1},{3,2},{4,3},{5,4},{6,5},{7,6},{8,7},{9,8},{10,9},{11,1... | collective-permute-start | bytes 196616 | tf_op jit(solution)/shard_map/ppermute | solution.py:19
  43.3 0.3 convolution_bitcast_fusion.2
  43.6 5.8 %collective-permute-start.11 = (bf16[1,2,4,64,256]{4,3,2,1,0:T(8,128)(2,1)S(1)}, bf16[1,2,4,64,256]{4,3,2,1,0:T(8,128)(2,1)S(1)}, u32[]{:S(2)}, u32[]{:S(2)}) collective-permute-start(bf16[1,2,4,64,256]{4,3,2,1,0:T(8,128)(2,1)S(1)} %bitcast.463), channel_id=1, source_target_pairs={{0,16},{16,32},{32,48},{48,64},{64,80},{80,96},{96,112},{1,17},{17... | collective-permute-start | bytes 786440 | tf_op jit(solution)/shard_map/ppermute | solution.py:29
  49.5 0.3 fusion.54
  50.1 0.3 convolution_add_fusion.15
  50.3 0.3 convolution_add_fusion.14
  50.6 0.3 convolution_add_fusion.13
  51.4 0.3 convolution_add_fusion.10
  51.8 0.3 fusion.19
  52.1 1.9 %collective-permute-start.8 = (bf16[1,2,4,64,256]{4,3,2,1,0:T(8,128)(2,1)S(1)}, bf16[1,2,4,64,256]{4,3,2,1,0:T(8,128)(2,1)S(1)}, u32[]{:S(2)}, u32[]{:S(2)}) collective-permute-start(bf16[1,2,4,64,256]{4,3,2,1,0:T(8,128)(2,1)S(1)} %fusion.19), channel_id=1, source_target_pairs={{16,0},{32,16},{48,32},{64,48},{80,64},{96,80},{112,96},{17,1},{33... | collective-permute-start | bytes 786440 | tf_op jit(solution)/shard_map/ppermute | solution.py:29
  54.1 0.3 convolution_bitcast_fusion.1
  54.9 1.0 fusion.21
  55.9 4.8 %collective-permute-done.8 = bf16[1,2,4,64,256]{4,3,2,1,0:T(8,128)(2,1)S(1)} collective-permute-done((bf16[1,2,4,64,256]{4,3,2,1,0:T(8,128)(2,1)S(1)}, bf16[1,2,4,64,256]{4,3,2,1,0:T(8,128)(2,1)S(1)}, u32[]{:S(2)}, u32[]{:S(2)}) %collective-permute-start.8) | collective-permute-done | bytes 262176 | tf_op jit(solution)/shard_map/ppermute | solution.py:29
  60.7 0.3 fusion.110
  61.1 0.3 convolution_add_fusion.8
  61.4 0.3 fusion.23
  61.8 4.8 %collective-permute-start.9 = (bf16[1,2,1,64,256]{4,3,2,1,0:T(8,128)(2,1)S(1)}, bf16[1,2,1,64,256]{4,3,2,1,0:T(8,128)(2,1)S(1)}, u32[]{:S(2)}, u32[]{:S(2)}) collective-permute-start(bf16[1,2,1,64,256]{4,3,2,1,0:T(8,128)(2,1)S(1)} %get-tuple-element.13), channel_id=1, source_target_pairs={{0,1},{1,2},{2,3},{3,4},{4,5},{5,6},{6,7},{7,8},{8,9},{9,10},{10,1... | collective-permute-start | bytes 196616 | tf_op jit(solution)/shard_map/ppermute | solution.py:17
  66.6 1.3 %collective-permute-start.10 = (bf16[1,2,1,64,256]{4,3,2,1,0:T(8,128)(2,1)S(1)}, bf16[1,2,1,64,256]{4,3,2,1,0:T(8,128)(2,1)S(1)}, u32[]{:S(2)}, u32[]{:S(2)}) collective-permute-start(bf16[1,2,1,64,256]{4,3,2,1,0:T(8,128)(2,1)S(1)} %get-tuple-element.14), channel_id=1, source_target_pairs={{1,0},{2,1},{3,2},{4,3},{5,4},{6,5},{7,6},{8,7},{9,8},{10,9},{11,1... | collective-permute-start | bytes 196616 | tf_op jit(solution)/shard_map/ppermute | solution.py:19
  67.9 0.3 convolution_bitcast_fusion.5
  68.2 0.3 convolution_bitcast_fusion.4
  68.5 0.3 convolution_bitcast_fusion.3
  68.9 36.9 %shard_map.76 = f32[96,256]{1,0:T(8,128)S(1)} custom-call(f32[1536,256]{1,0:T(8,128)S(1)} %pad_maximum_fusion.part_ref), custom_call_target="tpu_custom_call" | custom-call | tf_op jit(solution)/shard_map/pallas_call | solution.py:250
  106.0 0.3 fusion.46
  106.5 0.3 convolution_add_fusion.6
  107.1 0.3 convolution_add_fusion.4
  107.3 0.3 convolution_add_fusion.3
  107.6 0.3 convolution_add_fusion.2
  107.9 0.3 convolution_add_fusion.1
  108.1 1.0 fusion.18
  109.1 0.6 copy.40
  (68 shorter events, 7.8 us)
Async XLA Ops:
  0.6 16.9 %copy-start = (bf16[2,9,256,256]{3,2,1,0:T(8,128)(2,1)S(1)}, bf16[2,9,256,256]{3,2,1,0:T(8,128)(2,1)}, u32[]{:S(2)}) copy-start(bf16[2,9,256,256]{3,2,1,0:T(8,128)(2,1)} %param.7) | copy-start | bytes 7077892
  0.6 17.2 %copy-start.1 = (bf16[1,2,4,64,256]{4,3,2,1,0:T(8,128)(2,1)S(1)}, bf16[1,2,4,64,256]{4,3,2,1,0:T(8,128)(2,1)}, u32[]{:S(2)}) copy-start(bf16[1,2,4,64,256]{4,3,2,1,0:T(8,128)(2,1)} %param.5) | copy-start | bytes 786436
  1.7 13.6 %collective-permute-start.1 = (bf16[1,2,1,64,256]{4,3,2,1,0:T(8,128)(2,1)S(1)}, bf16[1,2,1,64,256]{4,3,2,1,0:T(8,128)(2,1)S(1)}, u32[]{:S(2)}, u32[]{:S(2)}) collective-permute-start(bf16[1,2,1,64,256]{4,3,2,1,0:T(8,128)(2,1)S(1)} %get-tuple-element.19), channel_id=1, source_target_pairs={{0,1},{1,2},{2,3},{3,4},{4,5},{5,6},{6,7},{7,8},{8,9},{9,10},{10,1... | collective-permute-start | bytes 196616 | tf_op jit(solution)/shard_map/ppermute | solution.py:17
  6.1 9.3 %collective-permute-start.2 = (bf16[1,2,1,64,256]{4,3,2,1,0:T(8,128)(2,1)S(1)}, bf16[1,2,1,64,256]{4,3,2,1,0:T(8,128)(2,1)S(1)}, u32[]{:S(2)}, u32[]{:S(2)}) collective-permute-start(bf16[1,2,1,64,256]{4,3,2,1,0:T(8,128)(2,1)S(1)} %get-tuple-element.20), channel_id=1, source_target_pairs={{1,0},{2,1},{3,2},{4,3},{5,4},{6,5},{7,6},{8,7},{9,8},{10,9},{11,1... | collective-permute-start | bytes 196616 | tf_op jit(solution)/shard_map/ppermute | solution.py:19
  7.4 14.4 %collective-permute-start = (bf16[1,2,4,64,256]{4,3,2,1,0:T(8,128)(2,1)}, bf16[1,2,4,64,256]{4,3,2,1,0:T(8,128)(2,1)S(1)}, u32[]{:S(2)}, u32[]{:S(2)}) collective-permute-start(bf16[1,2,4,64,256]{4,3,2,1,0:T(8,128)(2,1)} %param.9), channel_id=1, source_target_pairs={{16,0},{32,16},{48,32},{64,48},{80,64},{96,80},{112,96},{17,1},{33... | collective-permute-start | bytes 786440 | tf_op jit(solution)/shard_map/ppermute | solution.py:29
  19.0 2.5 %copy-start.2 = (bf16[2,3,256,256]{3,2,1,0:T(8,128)(2,1)S(1)}, bf16[2,3,256,256]{3,2,1,0:T(8,128)(2,1)}, u32[]{:S(2)}) copy-start(bf16[2,3,256,256]{3,2,1,0:T(8,128)(2,1)} %param.8) | copy-start | bytes 2359300
  19.6 5.2 %collective-permute-start.3 = (bf16[1,2,4,64,256]{4,3,2,1,0:T(8,128)(2,1)S(1)}, bf16[1,2,4,64,256]{4,3,2,1,0:T(8,128)(2,1)S(1)}, u32[]{:S(2)}, u32[]{:S(2)}) collective-permute-start(bf16[1,2,4,64,256]{4,3,2,1,0:T(8,128)(2,1)S(1)} %bitcast.460), channel_id=1, source_target_pairs={{0,16},{16,32},{32,48},{48,64},{64,80},{80,96},{96,112},{1,17},{17... | collective-permute-start | bytes 786440 | tf_op jit(solution)/shard_map/ppermute | solution.py:29
  25.3 5.9 %collective-permute-start.4 = (bf16[1,2,1,64,256]{4,3,2,1,0:T(8,128)(2,1)S(1)}, bf16[1,2,1,64,256]{4,3,2,1,0:T(8,128)(2,1)S(1)}, u32[]{:S(2)}, u32[]{:S(2)}) collective-permute-start(bf16[1,2,1,64,256]{4,3,2,1,0:T(8,128)(2,1)S(1)} %get-tuple-element.17), channel_id=1, source_target_pairs={{0,1},{1,2},{2,3},{3,4},{4,5},{5,6},{6,7},{7,8},{8,9},{9,10},{10,1... | collective-permute-start | bytes 196616 | tf_op jit(solution)/shard_map/ppermute | solution.py:17
  29.6 5.0 %collective-permute-start.5 = (bf16[1,2,1,64,256]{4,3,2,1,0:T(8,128)(2,1)S(1)}, bf16[1,2,1,64,256]{4,3,2,1,0:T(8,128)(2,1)S(1)}, u32[]{:S(2)}, u32[]{:S(2)}) collective-permute-start(bf16[1,2,1,64,256]{4,3,2,1,0:T(8,128)(2,1)S(1)} %get-tuple-element.18), channel_id=1, source_target_pairs={{1,0},{2,1},{3,2},{4,3},{5,4},{6,5},{7,6},{8,7},{9,8},{10,9},{11,1... | collective-permute-start | bytes 196616 | tf_op jit(solution)/shard_map/ppermute | solution.py:19
  37.5 11.9 %collective-permute-start.6 = (bf16[1,2,1,64,256]{4,3,2,1,0:T(8,128)(2,1)S(1)}, bf16[1,2,1,64,256]{4,3,2,1,0:T(8,128)(2,1)S(1)}, u32[]{:S(2)}, u32[]{:S(2)}) collective-permute-start(bf16[1,2,1,64,256]{4,3,2,1,0:T(8,128)(2,1)S(1)} %get-tuple-element.15), channel_id=1, source_target_pairs={{0,1},{1,2},{2,3},{3,4},{4,5},{5,6},{6,7},{7,8},{8,9},{9,10},{10,1... | collective-permute-start | bytes 196616 | tf_op jit(solution)/shard_map/ppermute | solution.py:17
  42.0 7.4 %collective-permute-start.7 = (bf16[1,2,1,64,256]{4,3,2,1,0:T(8,128)(2,1)S(1)}, bf16[1,2,1,64,256]{4,3,2,1,0:T(8,128)(2,1)S(1)}, u32[]{:S(2)}, u32[]{:S(2)}) collective-permute-start(bf16[1,2,1,64,256]{4,3,2,1,0:T(8,128)(2,1)S(1)} %get-tuple-element.16), channel_id=1, source_target_pairs={{1,0},{2,1},{3,2},{4,3},{5,4},{6,5},{7,6},{8,7},{9,8},{10,9},{11,1... | collective-permute-start | bytes 196616 | tf_op jit(solution)/shard_map/ppermute | solution.py:19
  43.6 10.5 %collective-permute-start.11 = (bf16[1,2,4,64,256]{4,3,2,1,0:T(8,128)(2,1)S(1)}, bf16[1,2,4,64,256]{4,3,2,1,0:T(8,128)(2,1)S(1)}, u32[]{:S(2)}, u32[]{:S(2)}) collective-permute-start(bf16[1,2,4,64,256]{4,3,2,1,0:T(8,128)(2,1)S(1)} %bitcast.463), channel_id=1, source_target_pairs={{0,16},{16,32},{32,48},{48,64},{64,80},{80,96},{96,112},{1,17},{17... | collective-permute-start | bytes 786440 | tf_op jit(solution)/shard_map/ppermute | solution.py:29
  50.9 1.0 copy-start.3
  52.1 8.6 %collective-permute-start.8 = (bf16[1,2,4,64,256]{4,3,2,1,0:T(8,128)(2,1)S(1)}, bf16[1,2,4,64,256]{4,3,2,1,0:T(8,128)(2,1)S(1)}, u32[]{:S(2)}, u32[]{:S(2)}) collective-permute-start(bf16[1,2,4,64,256]{4,3,2,1,0:T(8,128)(2,1)S(1)} %fusion.19), channel_id=1, source_target_pairs={{16,0},{32,16},{48,32},{64,48},{80,64},{96,80},{112,96},{17,1},{33... | collective-permute-start | bytes 786440 | tf_op jit(solution)/shard_map/ppermute | solution.py:29
  61.8 44.1 %collective-permute-start.9 = (bf16[1,2,1,64,256]{4,3,2,1,0:T(8,128)(2,1)S(1)}, bf16[1,2,1,64,256]{4,3,2,1,0:T(8,128)(2,1)S(1)}, u32[]{:S(2)}, u32[]{:S(2)}) collective-permute-start(bf16[1,2,1,64,256]{4,3,2,1,0:T(8,128)(2,1)S(1)} %get-tuple-element.13), channel_id=1, source_target_pairs={{0,1},{1,2},{2,3},{3,4},{4,5},{5,6},{6,7},{7,8},{8,9},{9,10},{10,1... | collective-permute-start | bytes 196616 | tf_op jit(solution)/shard_map/ppermute | solution.py:17
  66.6 39.3 %collective-permute-start.10 = (bf16[1,2,1,64,256]{4,3,2,1,0:T(8,128)(2,1)S(1)}, bf16[1,2,1,64,256]{4,3,2,1,0:T(8,128)(2,1)S(1)}, u32[]{:S(2)}, u32[]{:S(2)}) collective-permute-start(bf16[1,2,1,64,256]{4,3,2,1,0:T(8,128)(2,1)S(1)} %get-tuple-element.14), channel_id=1, source_target_pairs={{1,0},{2,1},{3,2},{4,3},{5,4},{6,5},{7,6},{8,7},{9,8},{10,9},{11,1... | collective-permute-start | bytes 196616 | tf_op jit(solution)/shard_map/ppermute | solution.py:19

commit v2 on v1

v2 whole, which is shorter than its diff:
```python
import jax
import jax.numpy as jnp
from jax import lax
from jax.experimental import pallas as pl
from jax.experimental.pallas import tpu as pltpu
from jax.sharding import PartitionSpec as P

XS, YS, CORES, ZS = 4, 4, 2, 16
TS = YS * CORES
CHIPS = XS * YS
PLANE = CHIPS * CORES
PIECE = 6
HALF = 128
C = 256
COLS = 64
ROWS = 4
OWN = 2
CELLS = OWN * ROWS * COLS
FRAMES = TS * OWN
BF, F32 = jnp.bfloat16, jnp.float32
NT = (((1,), (1,)), ((), ()))


def mm(left, right):
    return jnp.dot(left, right, preferred_element_type=F32)


def mm_nt(left, right):
    return lax.dot_general(left, right, NT, preferred_element_type=F32)


def rows_of(padded, first):
    return padded[:, first : first + ROWS].reshape(CELLS, C)


def shifted(values, by):
    column = lax.broadcasted_iota(jnp.int32, values.shape, 0) % COLS
    edge = 0 if by == 1 else COLS - 1
    return jnp.where(column == edge, 0.0, pltpu.roll(values, by % CELLS, 0))


def spatial(padded, weights):
    sums = []
    for kx in range(3):
        left = jnp.concatenate([rows_of(padded, ky) for ky in range(3)], axis=1)
        right = jnp.concatenate([weights[ky, kx] for ky in range(3)], axis=0)
        sums.append(mm(left, right))
    return shifted(sums[0], 1) + sums[1] + shifted(sums[2], -1)


def spatial_back(padded, weights):
    sums = []
    for kx in range(3):
        total = None
        for ky in range(3):
            part = mm_nt(rows_of(padded, 2 - ky), weights[ky, kx])
            total = part if total is None else total + part
        sums.append(total)
    return shifted(sums[0], -1) + sums[1] + shifted(sums[2], 1)


def kernel(
    seg, clips, space_w, time_w, upstream,
    grad_out, feat_out, weight_out,
    ws, wt, xh, acts, slopes, grads, dh, dact, turned, part, feat, gin,
    arranged, send_pair, recv_pair, send_plane, recv_plane, send_z, recv_z, total, recv_all, result,
    load, halo_s, halo_r, time_s, time_r, sums, store,
):
    x = lax.axis_index("dp")
    t = lax.axis_index("tm")
    z = lax.axis_index("rows")
    core = t % CORES
    chip = x * YS + t // CORES
    place = x * TS + t

    def plane_id(other):
        return {"dp": other // TS, "tm": other % TS}

    def chip_id(other):
        return {"dp": other // YS, "tm": (other % YS) * CORES + core}

    barrier = pltpu.get_barrier_semaphore()

    @pl.loop(1, PLANE)
    def _(step):
        pl.semaphore_signal(barrier, inc=1, device_id=plane_id((place + step) % PLANE))

    @pl.loop(1, ZS)
    def _(step):
        pl.semaphore_signal(barrier, inc=1, device_id={"rows": (z + step) % ZS})

    loads = [
        pltpu.make_async_copy(clips, xh.at[0, :, pl.ds(1, ROWS)], load.at[0]),
        pltpu.make_async_copy(space_w.at[0], ws.at[0], load.at[1]),
        pltpu.make_async_copy(time_w, wt, load.at[2]),
        pltpu.make_async_copy(upstream, grads.at[1, pl.ds(0, OWN)], load.at[3]),
        pltpu.make_async_copy(space_w.at[1], ws.at[1], load.at[4]),
    ]
    for copy in loads:
        copy.start()

    blank_row = jnp.zeros((OWN, COLS, C), BF)
    blank = jnp.zeros((OWN, ROWS, COLS, C), BF)

    @pl.when(z == 0)
    def _():
        for layer in range(2):
            xh[layer, :, 0] = blank_row
            dh[layer, :, 0] = blank_row

    @pl.when(z == ZS - 1)
    def _():
        for layer in range(2):
            xh[layer, :, ROWS + 1] = blank_row
            dh[layer, :, ROWS + 1] = blank_row

    @pl.when(t == 0)
    def _():
        for layer in range(2):
            acts[layer, :OWN] = blank

    @pl.when(t == TS - 1)
    def _():
        for layer in range(2):
            grads[layer, OWN:] = blank

    def halo(number, low, high, buffer):
        up = pltpu.make_async_remote_copy(
            src_ref=high, dst_ref=buffer.at[:, 0], send_sem=halo_s.at[number, 0], recv_sem=halo_r.at[number, 0],
            device_id={"rows": jnp.minimum(z + 1, ZS - 1)},
        )
        down = pltpu.make_async_remote_copy(
            src_ref=low, dst_ref=buffer.at[:, ROWS + 1], send_sem=halo_s.at[number, 1], recv_sem=halo_r.at[number, 1],
            device_id={"rows": jnp.maximum(z - 1, 0)},
        )
        return up, down

    def halo_start(pair):
        pl.when(z < ZS - 1)(pair[0].start)
        pl.when(z > 0)(pair[1].start)

    def halo_arrived(pair):
        pl.when(z > 0)(pair[0].wait_recv)
        pl.when(z < ZS - 1)(pair[1].wait_recv)

    def halo_sent(pair):
        pl.when(z < ZS - 1)(pair[0].wait_send)
        pl.when(z > 0)(pair[1].wait_send)

    def later(number, source, target):
        return pltpu.make_async_remote_copy(
            src_ref=source, dst_ref=target, send_sem=time_s.at[number], recv_sem=time_r.at[number],
            device_id={"tm": jnp.minimum(t + 1, TS - 1)},
        )

    def earlier(number, source, target):
        return pltpu.make_async_remote_copy(
            src_ref=source, dst_ref=target, send_sem=time_s.at[number], recv_sem=time_r.at[number],
            device_id={"tm": jnp.maximum(t - 1, 0)},
        )

    x_halo = [
        halo(0, clips.at[:, 0], clips.at[:, ROWS - 1], xh.at[0]),
        halo(1, xh.at[1, :, 1], xh.at[1, :, ROWS], xh.at[1]),
    ]
    d_halo = [
        halo(2, dh.at[0, :, 1], dh.at[0, :, ROWS], dh.at[0]),
        halo(3, dh.at[1, :, 1], dh.at[1, :, ROWS], dh.at[1]),
    ]
    act_copy = [later(layer, acts.at[layer, pl.ds(OWN, OWN)], acts.at[layer, pl.ds(0, OWN)]) for layer in range(2)]
    grad_copy = [
        earlier(2, grads.at[0, pl.ds(0, OWN)], grads.at[0, pl.ds(OWN, OWN)]),
        earlier(3, upstream, grads.at[1, pl.ds(OWN, OWN)]),
    ]

    def one_clip(frame, offset):
        first = jnp.maximum(frame - offset, 0)
        same = (frame - offset >= 0) & (frame < FRAMES) & (seg[0, first] == seg[0, jnp.minimum(frame, FRAMES - 1)])
        return jnp.where(same, 1.0, 0.0)

    first_frame = t * OWN
    back_mask = [[one_clip(first_frame + i, k) for i in range(OWN)] for k in range(3)]
    next_mask = [[one_clip(first_frame + i + k, k) for i in range(OWN)] for k in range(3)]

    def gated(values, mask):
        return (values.astype(F32) * mask).astype(BF)

    def temporal(layer):
        columns = []
        for k in range(3):
            frames = [acts[layer, OWN + i - k] for i in range(OWN)]
            if k:
                frames = [gated(frames[i], back_mask[k][i]) for i in range(OWN)]
            columns.append(jnp.stack(frames).reshape(CELLS, C))
        out = mm(jnp.concatenate(columns, axis=1), wt[layer].reshape(3 * C, C))
        return (xh[layer, :, 1 : ROWS + 1].astype(F32) + out.reshape(OWN, ROWS, COLS, C)).astype(BF)

    def lifted(layer, k):
        frames = [grads[layer, i + k] for i in range(OWN)]
        if k:
            frames = [gated(frames[i], next_mask[k][i]) for i in range(OWN)]
        return jnp.stack(frames).reshape(CELLS, C)

    def activate(layer):
        pre = spatial(xh.at[layer], ws.at[layer])
        sigma = jax.nn.sigmoid(pre)
        acts[layer, OWN:] = (pre * sigma).astype(BF).reshape(OWN, ROWS, COLS, C)
        slopes[layer] = sigma * (1.0 + pre * (1.0 - sigma))

    def grad_of_act(layer):
        out = mm_nt(lifted(layer, 0), wt[layer, 0])
        for k in range(1, 3):
            out = out + mm_nt(lifted(layer, k), wt[layer, k])
        return out

    pl.semaphore_wait(barrier, PLANE - 1 + ZS - 1)
    halo_start(x_halo[0])
    pl.when(t > 0)(grad_copy[1].start)

    loads[0].wait()
    loads[1].wait()
    halo_arrived(x_halo[0])
    activate(0)
    pl.when(t < TS - 1)(act_copy[0].start)
    for i in range(OWN):
        turned[:, (OWN + i) * 256 : (OWN + i + 1) * 256] = acts[0, OWN + i].reshape(256, C).T
    loads[2].wait()
    loads[3].wait()
    loads[4].wait()
    pl.when(t < TS - 1)(grad_copy[1].wait_recv)
    dact[...] = grad_of_act(1)

    pl.when(t > 0)(act_copy[0].wait_recv)
    xh[1, :, 1 : ROWS + 1] = temporal(0)
    halo_start(x_halo[1])
    for i in range(OWN):
        turned[:, i * 256 : (i + 1) * 256] = acts[0, i].reshape(256, C).T
    halo_arrived(x_halo[1])

    activate(1)
    dh[1, :, 1 : ROWS + 1] = (dact[...] * slopes[1]).astype(BF).reshape(OWN, ROWS, COLS, C)
    halo_start(d_halo[1])
    pl.when(t < TS - 1)(act_copy[1].start)
    own_turned = acts[1, OWN:].reshape(CELLS, C).T
    for k in range(3):
        part[(3 + k) * C : (4 + k) * C] = mm(own_turned, lifted(1, k))
    halo_arrived(d_halo[1])

    back = spatial_back(dh.at[1], ws.at[1])
    first_grad = grads[1, :OWN].reshape(CELLS, C).astype(F32) + back
    grads[0, :OWN] = first_grad.astype(BF).reshape(OWN, ROWS, COLS, C)
    pl.when(t > 0)(grad_copy[0].start)
    for k in range(3):
        frames = [grads[0, i] for i in range(OWN)]
        if k:
            frames = [gated(frames[i], back_mask[k][i]) for i in range(OWN)]
        part[k * C : (k + 1) * C] = mm(
            turned[:, (OWN - k) * 256 : (2 * OWN - k) * 256], jnp.stack(frames).reshape(CELLS, C)
        )

    @pl.loop(0, XS)
    def _(high):
        for block in range(ZS):
            rows = part[pl.ds(pl.multiple_of(96 * block + PIECE * YS * high, 8), PIECE * YS), :]
            for low in range(YS):
                arranged[high * YS + low, PIECE * block : PIECE * (block + 1), :] = rows[
                    PIECE * low : PIECE * (low + 1)
                ]

    @pl.loop(0, CHIPS)
    def _(group):
        rows = arranged[group]
        other = jnp.where(core == 0, rows[:, HALF:], rows[:, :HALF])
        send_pair[group] = other.astype(BF)

    pair = pltpu.make_async_remote_copy(
        src_ref=send_pair, dst_ref=recv_pair, send_sem=sums.at[0], recv_sem=sums.at[1],
        device_id={"tm": t + 1 - 2 * core},
    )
    pair.start()
    pair.wait()

    @pl.loop(0, CHIPS)
    def _(group):
        rows = arranged[group]
        own = jnp.where(core == 0, rows[:, :HALF], rows[:, HALF:])
        send_plane[group] = (own + recv_pair[group].astype(F32)).astype(BF)

    @pl.loop(1, CHIPS)
    def _(step):
        other = (chip + step) % CHIPS
        pltpu.make_async_remote_copy(
            src_ref=send_plane.at[other], dst_ref=recv_plane.at[chip], send_sem=sums.at[2], recv_sem=sums.at[3],
            device_id=chip_id(other),
        ).start()

    recv_plane[chip] = send_plane[chip]

    pl.when(t < TS - 1)(grad_copy[0].wait_recv)
    dh[0, :, 1 : ROWS + 1] = (grad_of_act(0) * slopes[0]).astype(BF).reshape(OWN, ROWS, COLS, C)
    halo_start(d_halo[0])

    pltpu.make_async_remote_copy(
        src_ref=send_plane.at[pl.ds(0, CHIPS - 1)], dst_ref=recv_plane.at[pl.ds(0, CHIPS - 1)],
        send_sem=sums.at[2], recv_sem=sums.at[3], device_id=chip_id((chip + 1) % CHIPS),
    ).wait()
    summed = recv_plane[0].astype(F32)
    for group in range(1, CHIPS):
        summed = summed + recv_plane[group].astype(F32)
    for block in range(ZS):
        send_z[block, :PIECE, :] = summed[PIECE * block : PIECE * (block + 1), :]
        send_z[block, PIECE:, :] = jnp.zeros((8 - PIECE, HALF), F32)

    @pl.loop(1, ZS)
    def _(step):
        other = (z + step) % ZS
        pltpu.make_async_remote_copy(
            src_ref=send_z.at[other], dst_ref=recv_z.at[z], send_sem=sums.at[4], recv_sem=sums.at[5],
            device_id={"rows": other},
        ).start()

    recv_z[z] = send_z[z]

    pl.when(t > 0)(act_copy[1].wait_recv)
    feat[...] = temporal(1)
    feat_store = pltpu.make_async_copy(feat, feat_out, store.at[0])
    feat_store.start()
    halo_arrived(d_halo[0])
    gin[...] = (grads[0, :OWN].reshape(CELLS, C).astype(F32) + spatial_back(dh.at[0], ws.at[0])).astype(BF).reshape(
        OWN, ROWS, COLS, C
    )
    gin_store = pltpu.make_async_copy(gin, grad_out, store.at[1])
    gin_store.start()

    pltpu.make_async_remote_copy(
        src_ref=send_z.at[pl.ds(0, ZS - 1)], dst_ref=recv_z.at[pl.ds(0, ZS - 1)],
        send_sem=sums.at[4], recv_sem=sums.at[5], device_id={"rows": (z + 1) % ZS},
    ).wait()
    final = recv_z[0]
    for block in range(1, ZS):
        final = final + recv_z[block]
    total[...] = final

    @pl.loop(1, PLANE)
    def _(step):
        pltpu.make_async_remote_copy(
            src_ref=total, dst_ref=recv_all.at[place], send_sem=sums.at[6], recv_sem=sums.at[7],
            device_id=plane_id((place + step) % PLANE),
        ).start()

    recv_all[place] = final
    for pair in x_halo + d_halo:
        halo_sent(pair)
    for copy in act_copy:
        pl.when(t < TS - 1)(copy.wait_send)
    for copy in grad_copy:
        pl.when(t > 0)(copy.wait_send)
    feat_store.wait()
    gin_store.wait()
    pltpu.make_async_remote_copy(
        src_ref=recv_all.at[pl.ds(0, PLANE - 1)], dst_ref=recv_all.at[pl.ds(0, PLANE - 1)],
        send_sem=sums.at[6], recv_sem=sums.at[7], device_id=plane_id((place + 1) % PLANE),
    ).wait()
    for group in range(CHIPS):
        for half in range(CORES):
            result[PIECE * group : PIECE * (group + 1), HALF * half : HALF * (half + 1)] = recv_all[
                group * CORES + half, :PIECE, :
            ]
    weight_store = pltpu.make_async_copy(result, weight_out, store.at[2])
    weight_store.start()
    weight_store.wait()


def local(clips, segment_ids, spatial_weight, temporal_weight, upstream):
    deep = PIECE * ZS
    cells = (OWN, ROWS, COLS, C)
    anywhere = pl.BlockSpec(memory_space=pl.ANY)
    grad, features, weight_grad = pl.pallas_call(
        kernel,
        out_shape=(
            jax.ShapeDtypeStruct(cells, BF),
            jax.ShapeDtypeStruct(cells, BF),
            jax.ShapeDtypeStruct((6 * C // ZS, C), F32),
        ),
        in_specs=[pl.BlockSpec(memory_space=pltpu.SMEM)] + [anywhere] * 4,
        out_specs=(anywhere,) * 3,
        scratch_shapes=[
            pltpu.VMEM((2, 3, 3, C, C), BF),
            pltpu.VMEM((2, 3, C, C), BF),
            pltpu.VMEM((2, OWN, ROWS + 2, COLS, C), BF),
            pltpu.VMEM((2, 2 * OWN, ROWS, COLS, C), BF),
            pltpu.VMEM((2, CELLS, C), F32),
            pltpu.VMEM((2, 2 * OWN, ROWS, COLS, C), BF),
            pltpu.VMEM((2, OWN, ROWS + 2, COLS, C), BF),
            pltpu.VMEM((CELLS, C), F32),
            pltpu.VMEM((C, 2 * CELLS), BF),
            pltpu.VMEM((6 * C, C), F32),
            pltpu.VMEM(cells, BF),
            pltpu.VMEM(cells, BF),
            pltpu.VMEM((CHIPS, deep, C), F32),
            pltpu.VMEM((CHIPS, deep, HALF), BF),
            pltpu.VMEM((CHIPS, deep, HALF), BF),
            pltpu.VMEM((CHIPS, deep, HALF), BF),
            pltpu.VMEM((CHIPS, deep, HALF), BF),
            pltpu.VMEM((ZS, 8, HALF), F32),
            pltpu.VMEM((ZS, 8, HALF), F32),
            pltpu.VMEM((8, HALF), F32),
            pltpu.VMEM((PLANE, 8, HALF), F32),
            pltpu.VMEM((6 * C // ZS, C), F32),
            pltpu.SemaphoreType.DMA((5,)),
            pltpu.SemaphoreType.DMA((4, 2)),
            pltpu.SemaphoreType.DMA((4, 2)),
            pltpu.SemaphoreType.DMA((4,)),
            pltpu.SemaphoreType.DMA((4,)),
            pltpu.SemaphoreType.DMA((8,)),
            pltpu.SemaphoreType.DMA((3,)),
        ],
        compiler_params=pltpu.CompilerParams(
            collective_id=0, has_side_effects=True, vmem_limit_bytes=56 * 1024 * 1024
        ),
    )(
        segment_ids,
        clips.reshape(cells),
        spatial_weight.reshape(2, 3, 3, C, C),
        temporal_weight,
        upstream.reshape(cells),
    )
    return (grad.reshape(clips.shape), features.reshape(clips.shape), weight_grad)


def solution(mesh):
    return jax.shard_map(
        local,
        mesh=mesh,
        in_specs=(
            P("dp", "tm", "rows", None, None),
            P("dp", None),
            P(),
            P(),
            P("dp", "tm", "rows", None, None),
        ),
        out_specs=(
            P("dp", "tm", "rows", None, None),
            P("dp", "tm", "rows", None, None),
            P("rows", None),
        ),
        check_vma=False,
    )
```

time: 110 us -> 67.4 us (0.61)
  starting transfers between devices: 38.4 us -> 0 us
  Pallas kernels: 36.9 us -> 61.6 us
  matrix products: 16.2 us -> 0 us
  waiting for transfers between devices: 10.9 us -> 0 us
  other arithmetic: 3.15 us -> 0 us
  local copies, waits for them, and re-layouts: 2.86 us -> 4.88 us
    ppermute x12 -> x0, starting transfers between devices: 38.4 us -> none  [the longest x4 17.9 us: with_halo(): lax.ppermute(tail, axis, [(i, (i + 1) % count) for i in range(ends)])]
    pallas_call x1, Pallas kernels: 36.9 us -> 61.6 us  [local(): pl.pallas_call(kernel, out_shape=(jax.ShapeDtypeStruct(cells, BF), jax.Sh...]
    dot_general x54 -> x0, matrix products: 16.2 us -> none  [the longest x36 10.7 us: spatial_local(): jnp.dot(window.reshape(-1, channels), matrix, preferred_element_type=jnp....]
    ppermute x12 -> x0, waiting for transfers between devices: 10.9 us -> none  [the longest x4 7.45 us: from_behind(): lax.ppermute(value, axis, [(source, source + steps) for source in range(f...]
    unnamed x10 -> x3, local copies, waits for them, and re-layouts: 1.78 us -> 4.88 us
    concatenate x8 -> x0, other arithmetic: 1.79 us -> none  [the longest x4 1.45 us: with_halo(): jnp.concatenate([lax.ppermute(tail, axis, [(i, (i + 1) % count) for i in...]
  transfers between devices with their start and end apart: 12 -> 0, of which waited for: 3 -> 0; matrix products, arithmetic and copies ran while one was open for 12% -> 0% of each run, Pallas kernels for 34% -> 0%
where the time goes in v2:
time: 67.4 us; the launch traced here: 67.2 us
  Pallas kernels  61.6 us (91%)
  local copies, waits for them, and re-layouts  4.88 us (7%)
    pallas_call x1, Pallas kernels, local(): pl.pallas_call(kernel, out_shape=(jax.ShapeDtypeStruct(cells, BF), jax.Sh...  61.6 us
    unnamed x3, local copies, waits for them, and re-layouts  4.88 us

profile of v2, /device:TPU:1, one launch (start us, length us, event | category | flops | bytes accessed | tf_op | source)
XLA Modules:
  0.0 67.2 jit_solution(17286086174320990861)
XLA Ops:
  0.6 61.6 %shard_map.76 = (bf16[2,4,64,256]{3,2,1,0:T(8,128)(2,1)}, bf16[2,4,64,256]{3,2,1,0:T(8,128)(2,1)}, f32[96,256]{1,0:T(8,128)}) custom-call(s32[1,16]{1,0:T(1,128)} %seg.1, bf16[2,4,64,256]{3,2,1,0:T(8,128)(2,1)} %bitcast.8, bf16[2,3,3,256,256]{4,3,2,1,0:T(8,128)(2,1)} %bitcast.5, bf16[2,3,256,256]{3,2,1,0:T(8,128)(2,1)} %time_w.1, bf16[2,4,64,256]{3,2,1,0:T(8,128)(2,1)} %bitcast.9), custom_call_target="tpu_custom_call" | custom-call | tf_op jit(solution)/shard_map/pallas_call | solution.py:378
  62.3 1.7 %copy.11 = bf16[1,2,4,64,256]{4,3,2,1,0:T(8,128)(2,1)} copy(bf16[1,2,4,64,256]{4,3,2,1,0:T(8,128)(2,1)} %bitcast.7) | data formatting | bytes 524288
  63.9 1.7 %copy.12 = bf16[1,2,4,64,256]{4,3,2,1,0:T(8,128)(2,1)} copy(bf16[1,2,4,64,256]{4,3,2,1,0:T(8,128)(2,1)} %bitcast.6) | data formatting | bytes 524288
  65.6 1.5 %copy.13 = f32[96,256]{1,0:T(8,128)} copy(f32[96,256]{1,0:T(8,128)} %get-tuple-element.14) | data formatting | bytes 196608

commit v3 on v2

v3 whole, which is shorter than its diff:
```python
import jax
import jax.numpy as jnp
from jax import lax
from jax.experimental import pallas as pl
from jax.experimental.pallas import tpu as pltpu
from jax.sharding import PartitionSpec as P

XS, YS, CORES, ZS = 4, 4, 2, 16
TS = YS * CORES
CHIPS = XS * YS
PLANE = CHIPS * CORES
PIECE = 6
HALF = 128
C = 256
COLS = 64
ROWS = 4
OWN = 2
CELLS = OWN * ROWS * COLS
FRAMES = TS * OWN
DEEP = ZS // 2
BF, F32 = jnp.bfloat16, jnp.float32
NT = (((1,), (1,)), ((), ()))


def mm(left, right):
    return jnp.dot(left, right, preferred_element_type=F32)


def mm_nt(left, right):
    return lax.dot_general(left, right, NT, preferred_element_type=F32)


def rows_of(padded, first, rows):
    return padded[:, first : first + rows].reshape(OWN * rows * COLS, C)


def shifted(values, by):
    column = lax.broadcasted_iota(jnp.int32, values.shape, 0) % COLS
    edge = 0 if by == 1 else COLS - 1
    return jnp.where(column == edge, 0.0, pltpu.roll(values, by % values.shape[0], 0))


def spatial(padded, weights, rows):
    sums = []
    for kx in range(3):
        left = jnp.concatenate([rows_of(padded, ky, rows) for ky in range(3)], axis=1)
        right = jnp.concatenate([weights[ky, kx] for ky in range(3)], axis=0)
        sums.append(mm(left, right))
    return shifted(sums[0], 1) + sums[1] + shifted(sums[2], -1)


def spatial_back(padded, weights):
    sums = []
    for kx in range(3):
        total = None
        for ky in range(3):
            part = mm_nt(rows_of(padded, 2 - ky, ROWS), weights[ky, kx])
            total = part if total is None else total + part
        sums.append(total)
    return shifted(sums[0], -1) + sums[1] + shifted(sums[2], 1)


def finish(grad_in, feat_in, weight_in, grad_out, feat_out, weight_out, done):
    pairs = ((grad_in, grad_out), (feat_in, feat_out), (weight_in, weight_out))
    copies = [pltpu.make_async_copy(pair[0], pair[1], done.at[i]) for i, pair in enumerate(pairs)]
    for copy in copies:
        copy.start()
    for copy in copies:
        copy.wait()


def kernel(
    seg, clips, space_w, time_w, upstream,
    grad_out, feat_out, weight_out,
    ws, wt, x0, x1, act0, act1, slope0, slope1, g2, g1, dpre1, dpre0, dact, turned, part, feat, gin,
    arranged, send_pair, recv_pair, send_plane, recv_plane, send_z, recv_z, total, recv_all, result,
    load, wide_s, wide_r, near_s, near_r, sums, store, known,
):
    x = lax.axis_index("dp")
    t = lax.axis_index("tm")
    z = lax.axis_index("rows")
    core = t % CORES
    chip = x * YS + t // CORES
    place = x * TS + t

    def at(dx, dt, dz):
        return {"dp": (x + dx) % XS, "tm": (t + dt) % TS, "rows": (z + dz) % ZS}

    def plane_id(other):
        return {"dp": other // TS, "tm": other % TS}

    def chip_id(other):
        return {"dp": other // YS, "tm": (other % YS) * CORES + core}

    near = [(0, dt, dz) for dt in (-1, 0, 1) for dz in (-1, 0, 1) if dt or dz]
    near += [(-1, 0, 0), (1, 0, 0), (0, -2, 0), (0, 2, 0)]
    second = [(0, 0, -2), (0, 0, 2), (-1, 0, 0), (1, 0, 0), (2, 0, 0)]
    third = [(0, 0, -4), (0, 0, 4)]

    def tell(semaphore, partners):
        for partner in partners:
            pl.semaphore_signal(semaphore, inc=1, device_id=at(*partner))

    barrier = pltpu.get_barrier_semaphore()
    tell(barrier, near)

    loads = [
        pltpu.make_async_copy(clips, x0.at[pl.ds(OWN, OWN), pl.ds(3, ROWS)], load.at[0]),
        pltpu.make_async_copy(space_w.at[0], ws.at[0], load.at[1]),
        pltpu.make_async_copy(time_w, wt, load.at[2]),
        pltpu.make_async_copy(upstream, g2.at[pl.ds(0, OWN), pl.ds(1, ROWS)], load.at[3]),
        pltpu.make_async_copy(space_w.at[1], ws.at[1], load.at[4]),
    ]
    for copy in loads:
        copy.start()

    def blank(ref):
        ref[...] = jnp.zeros(ref.shape, ref.dtype)

    first, last = z == 0, z == ZS - 1
    early, late = t == 0, t == TS - 1

    @pl.when(first)
    def _():
        blank(x0.at[:, pl.ds(0, 3)])
        blank(g2.at[:, pl.ds(0, 1)])
        blank(dpre0.at[:, pl.ds(0, 1)])

    @pl.when(last)
    def _():
        blank(x0.at[:, pl.ds(ROWS + 3, 3)])
        blank(g2.at[:, pl.ds(ROWS + 1, 1)])
        blank(dpre0.at[:, pl.ds(ROWS + 1, 1)])

    @pl.when(early)
    def _():
        blank(x0.at[pl.ds(0, OWN)])
        blank(act1.at[pl.ds(0, OWN)])

    @pl.when(late)
    def _():
        blank(g2.at[pl.ds(OWN, OWN)])
        blank(g1.at[pl.ds(OWN, OWN)])

    def remote(source, target, sems_s, sems_r, number, dt, dz):
        copy = pltpu.make_async_remote_copy(
            src_ref=source, dst_ref=target, send_sem=sems_s.at[number], recv_sem=sems_r.at[number],
            device_id=at(0, dt, dz),
        )
        sends, takes = [], []
        if dt == 1:
            sends.append(t < TS - 1)
            takes.append(t > 0)
        if dt == -1:
            sends.append(t > 0)
            takes.append(t < TS - 1)
        if dz == 1:
            sends.append(z < ZS - 1)
            takes.append(z > 0)
        if dz == -1:
            sends.append(z > 0)
            takes.append(z < ZS - 1)
        send, take = sends[0], takes[0]
        for more in sends[1:]:
            send = send & more
        for more in takes[1:]:
            take = take & more
        return copy, send, take

    def start(group):
        for copy, send, _ in group:
            pl.when(send)(copy.start)

    def arrived(group):
        for copy, _, take in group:
            pl.when(take)(copy.wait_recv)

    def sent(group):
        for copy, send, _ in group:
            pl.when(send)(copy.wait_send)

    x_low, x_high = clips.at[:, pl.ds(0, 3)], clips.at[:, pl.ds(1, 3)]
    prior, own = pl.ds(0, OWN), pl.ds(OWN, OWN)
    top, middle, bottom = pl.ds(0, 3), pl.ds(3, ROWS), pl.ds(ROWS + 3, 3)
    x_halo = [
        remote(x_high, x0.at[own, top], wide_s, wide_r, 0, 0, 1),
        remote(x_low, x0.at[own, bottom], wide_s, wide_r, 1, 0, -1),
    ]
    x_prior = [remote(clips, x0.at[prior, middle], wide_s, wide_r, 2, 1, 0)]
    x_corner = [
        remote(x_high, x0.at[prior, top], wide_s, wide_r, 3, 1, 1),
        remote(x_low, x0.at[prior, bottom], wide_s, wide_r, 4, 1, -1),
    ]
    g_low, g_high = upstream.at[:, pl.ds(0, 1)], upstream.at[:, pl.ds(ROWS - 1, 1)]
    now, after = pl.ds(0, OWN), pl.ds(OWN, OWN)
    over, inner, under = pl.ds(0, 1), pl.ds(1, ROWS), pl.ds(ROWS + 1, 1)
    g_halo = [
        remote(g_high, g2.at[now, over], wide_s, wide_r, 5, 0, 1),
        remote(g_low, g2.at[now, under], wide_s, wide_r, 6, 0, -1),
        remote(upstream, g2.at[after, inner], wide_s, wide_r, 7, -1, 0),
        remote(g_high, g2.at[after, over], wide_s, wide_r, 8, -1, 1),
        remote(g_low, g2.at[after, under], wide_s, wide_r, 9, -1, -1),
    ]
    act_copy = [remote(act1.at[own], act1.at[prior], near_s, near_r, 0, 1, 0)]
    g1_copy = [remote(g1.at[now], g1.at[after], near_s, near_r, 1, -1, 0)]
    d_halo = [
        remote(dpre0.at[:, pl.ds(ROWS, 1)], dpre0.at[:, over], near_s, near_r, 2, 0, 1),
        remote(dpre0.at[:, pl.ds(1, 1)], dpre0.at[:, under], near_s, near_r, 3, 0, -1),
    ]

    def one_clip(frame, offset):
        before = jnp.maximum(frame - offset, 0)
        same = (frame - offset >= 0) & (frame < FRAMES) & (seg[0, before] == seg[0, jnp.minimum(frame, FRAMES - 1)])
        return jnp.where(same, 1.0, 0.0)

    first_frame = t * OWN
    back_mask = [[one_clip(first_frame + i, k) for i in range(OWN)] for k in range(3)]
    next_mask = [[one_clip(first_frame + i + k, k) for i in range(OWN)] for k in range(3)]

    def gated(values, mask):
        return (values.astype(F32) * mask).astype(BF)

    def temporal(base, acts, weights):
        rows = base.shape[1]
        columns = []
        for k in range(3):
            frames = [acts[OWN + i - k] for i in range(OWN)]
            if k:
                frames = [gated(frames[i], back_mask[k][i]) for i in range(OWN)]
            columns.append(jnp.stack(frames).reshape(OWN * rows * COLS, C))
        out = mm(jnp.concatenate(columns, axis=1), weights.reshape(3 * C, C))
        return (base.astype(F32) + out.reshape(base.shape)).astype(BF)

    def lifted(grads, k):
        frames = [grads[i + k] for i in range(OWN)]
        if k:
            frames = [gated(frames[i], next_mask[k][i]) for i in range(OWN)]
        return jnp.stack(frames).reshape(OWN * frames[0].shape[0] * COLS, C)

    def grad_of_act(grads, weights):
        out = mm_nt(lifted(grads, 0), weights[0])
        for k in range(1, 3):
            out = out + mm_nt(lifted(grads, k), weights[k])
        return out

    def slope(pre, sigma):
        return sigma * (1.0 + pre * (1.0 - sigma))

    pl.semaphore_wait(barrier, len(near))
    start(x_halo)
    start(x_prior)
    start(x_corner)
    tell(known.at[0], near)

    loads[0].wait()
    loads[1].wait()
    arrived(x_halo)
    start(g_halo)
    wide = (OWN, ROWS + 4, COLS, C)
    pre = spatial(x0.at[own], ws.at[0], ROWS + 4)
    sigma = jax.nn.sigmoid(pre)
    act0[OWN:] = (pre * sigma).astype(BF).reshape(wide)
    slope0[...] = slope(pre, sigma).reshape(wide)[:, 2 : ROWS + 2].reshape(CELLS, C)
    pl.semaphore_wait(known.at[0], len(near))
    tell(known.at[1], second)

    def turn(i):
        turned[:, i * 256 : (i + 1) * 256] = act0[i, 2 : ROWS + 2].reshape(256, C).T

    for i in range(OWN):
        turn(OWN + i)
    loads[2].wait()
    loads[3].wait()
    loads[4].wait()
    arrived(x_prior)
    arrived(x_corner)
    pre = spatial(x0.at[prior], ws.at[0], ROWS + 4)
    act0[:OWN] = (pre * jax.nn.sigmoid(pre)).astype(BF).reshape(wide)
    x1[...] = temporal(x0[OWN:, 1 : ROWS + 5], act0, wt[0])

    @pl.when(first)
    def _():
        blank(x1.at[:, pl.ds(0, 2)])

    @pl.when(last)
    def _():
        blank(x1.at[:, pl.ds(ROWS + 2, 2)])

    tall = (OWN, ROWS + 2, COLS, C)
    pre = spatial(x1, ws.at[1], ROWS + 2)
    sigma = jax.nn.sigmoid(pre)
    act1[OWN:] = (pre * sigma).astype(BF).reshape(tall)[:, 1 : ROWS + 1]
    slope1[...] = slope(pre, sigma)
    start(act_copy)
    arrived(g_halo)
    dact[...] = grad_of_act(g2, wt[1])
    dpre1[...] = (dact[...] * slope1[...]).astype(BF).reshape(tall)

    @pl.when(first)
    def _():
        blank(dpre1.at[:, over])

    @pl.when(last)
    def _():
        blank(dpre1.at[:, under])

    g1[:OWN] = (
        g2[:OWN, 1 : ROWS + 1].astype(F32) + spatial_back(dpre1, ws.at[1]).reshape(OWN, ROWS, COLS, C)
    ).astype(BF)
    start(g1_copy)
    for i in range(OWN):
        turn(i)
    for k in range(3):
        frames = [g1[i] for i in range(OWN)]
        if k:
            frames = [gated(frames[i], back_mask[k][i]) for i in range(OWN)]
        part[0, k * C : (k + 1) * C] = mm(
            turned[:, (OWN - k) * 256 : (2 * OWN - k) * 256], jnp.stack(frames).reshape(CELLS, C)
        )

    def pair_copy(layer):
        return pltpu.make_async_remote_copy(
            src_ref=send_pair.at[layer], dst_ref=recv_pair.at[layer], send_sem=sums.at[layer],
            recv_sem=sums.at[2 + layer], device_id={"tm": t + 1 - 2 * core},
        )

    def arrange(layer):
        @pl.loop(0, XS)
        def _(high):
            for block in range(DEEP):
                rows = part[layer, pl.ds(pl.multiple_of(96 * block + PIECE * YS * high, 8), PIECE * YS), :]
                for low in range(YS):
                    arranged[layer, high * YS + low, PIECE * block : PIECE * (block + 1), :] = rows[
                        PIECE * low : PIECE * (low + 1)
                    ]

        @pl.loop(0, CHIPS)
        def _(group):
            rows = arranged[layer, group]
            send_pair[layer, group] = jnp.where(core == 0, rows[:, HALF:], rows[:, :HALF]).astype(BF)

        pair_copy(layer).start()

    def spread(layer):
        pair_copy(layer).wait()

        @pl.loop(0, CHIPS)
        def _(group):
            rows = arranged[layer, group]
            mine = jnp.where(core == 0, rows[:, :HALF], rows[:, HALF:])
            send_plane[layer, group] = (mine + recv_pair[layer, group].astype(F32)).astype(BF)

        @pl.loop(1, CHIPS)
        def _(step):
            other = (chip + step) % CHIPS
            pltpu.make_async_remote_copy(
                src_ref=send_plane.at[layer, other], dst_ref=recv_plane.at[layer, chip],
                send_sem=sums.at[4 + layer], recv_sem=sums.at[6 + layer], device_id=chip_id(other),
            ).start()

        recv_plane[layer, chip] = send_plane[layer, chip]

    def gather(layer):
        pltpu.make_async_remote_copy(
            src_ref=send_plane.at[layer, pl.ds(0, CHIPS - 1)], dst_ref=recv_plane.at[layer, pl.ds(0, CHIPS - 1)],
            send_sem=sums.at[4 + layer], recv_sem=sums.at[6 + layer], device_id=chip_id((chip + 1) % CHIPS),
        ).wait()
        summed = recv_plane[layer, 0].astype(F32)
        for group in range(1, CHIPS):
            summed = summed + recv_plane[layer, group].astype(F32)
        for block in range(DEEP):
            send_z[layer * DEEP + block, :PIECE, :] = summed[PIECE * block : PIECE * (block + 1), :]
            send_z[layer * DEEP + block, PIECE:, :] = jnp.zeros((8 - PIECE, HALF), F32)

        @pl.loop(0, DEEP)
        def _(step):
            other = layer * DEEP + (z + step) % DEEP

            @pl.when(other != z)
            def _():
                pltpu.make_async_remote_copy(
                    src_ref=send_z.at[other], dst_ref=recv_z.at[z], send_sem=sums.at[8], recv_sem=sums.at[9],
                    device_id={"rows": other},
                ).start()

    arrange(0)
    turned_own = act1[OWN:].reshape(CELLS, C).T
    for k in range(3):
        frames = [g2[i + k, 1 : ROWS + 1] for i in range(OWN)]
        if k:
            frames = [gated(frames[i], next_mask[k][i]) for i in range(OWN)]
        part[1, k * C : (k + 1) * C] = mm(turned_own, jnp.stack(frames).reshape(CELLS, C))
    arrange(1)
    pl.semaphore_wait(known.at[1], len(second))
    tell(known.at[2], third)
    spread(0)
    spread(1)

    arrived(g1_copy)
    dpre0[:, 1 : ROWS + 1] = (grad_of_act(g1, wt[0]) * slope0[...]).astype(BF).reshape(OWN, ROWS, COLS, C)
    start(d_halo)
    pl.semaphore_wait(known.at[2], len(third))
    gather(0)
    gather(1)
    recv_z[z] = send_z[z]

    arrived(act_copy)
    feat[...] = temporal(x1[:, 2 : ROWS + 2], act1, wt[1])
    feat_store = pltpu.make_async_copy(feat, feat_out, store.at[0])
    feat_store.start()
    arrived(d_halo)
    gin[...] = (
        g1[:OWN].astype(F32) + spatial_back(dpre0, ws.at[0]).reshape(OWN, ROWS, COLS, C)
    ).astype(BF)
    gin_store = pltpu.make_async_copy(gin, grad_out, store.at[1])
    gin_store.start()

    pltpu.make_async_remote_copy(
        src_ref=send_z.at[pl.ds(0, ZS - 1)], dst_ref=recv_z.at[pl.ds(0, ZS - 1)],
        send_sem=sums.at[8], recv_sem=sums.at[9], device_id={"rows": (z + 1) % ZS},
    ).wait()
    final = recv_z[0]
    for block in range(1, ZS):
        final = final + recv_z[block]
    total[...] = final

    @pl.loop(1, PLANE)
    def _(step):
        pltpu.make_async_remote_copy(
            src_ref=total, dst_ref=recv_all.at[place], send_sem=sums.at[10], recv_sem=sums.at[11],
            device_id=plane_id((place + step) % PLANE),
        ).start()

    recv_all[place] = final
    for group in (x_halo, x_prior, x_corner, g_halo, act_copy, g1_copy, d_halo):
        sent(group)
    feat_store.wait()
    gin_store.wait()
    pltpu.make_async_remote_copy(
        src_ref=recv_all.at[pl.ds(0, PLANE - 1)], dst_ref=recv_all.at[pl.ds(0, PLANE - 1)],
        send_sem=sums.at[10], recv_sem=sums.at[11], device_id=plane_id((place + 1) % PLANE),
    ).wait()
    for group in range(CHIPS):
        for half in range(CORES):
            result[PIECE * group : PIECE * (group + 1), HALF * half : HALF * (half + 1)] = recv_all[
                group * CORES + half, :PIECE, :
            ]
    weight_store = pltpu.make_async_copy(result, weight_out, store.at[2])
    weight_store.start()
    weight_store.wait()


def local(clips, segment_ids, spatial_weight, temporal_weight, upstream):
    deep = PIECE * DEEP
    cells = (OWN, ROWS, COLS, C)
    anywhere = pl.BlockSpec(memory_space=pl.ANY)
    outs = (
        jax.ShapeDtypeStruct(cells, BF),
        jax.ShapeDtypeStruct(cells, BF),
        jax.ShapeDtypeStruct((6 * C // ZS, C), F32),
    )
    parts = pl.pallas_call(
        kernel,
        out_shape=outs,
        in_specs=[pl.BlockSpec(memory_space=pltpu.SMEM)] + [anywhere] * 4,
        out_specs=(anywhere,) * 3,
        scratch_shapes=[
            pltpu.VMEM((2, 3, 3, C, C), BF),
            pltpu.VMEM((2, 3, C, C), BF),
            pltpu.VMEM((2 * OWN, ROWS + 6, COLS, C), BF),
            pltpu.VMEM((OWN, ROWS + 4, COLS, C), BF),
            pltpu.VMEM((2 * OWN, ROWS + 4, COLS, C), BF),
            pltpu.VMEM((2 * OWN, ROWS, COLS, C), BF),
            pltpu.VMEM((CELLS, C), F32),
            pltpu.VMEM((OWN * (ROWS + 2) * COLS, C), F32),
            pltpu.VMEM((2 * OWN, ROWS + 2, COLS, C), BF),
            pltpu.VMEM((2 * OWN, ROWS, COLS, C), BF),
            pltpu.VMEM((OWN, ROWS + 2, COLS, C), BF),
            pltpu.VMEM((OWN, ROWS + 2, COLS, C), BF),
            pltpu.VMEM((OWN * (ROWS + 2) * COLS, C), F32),
            pltpu.VMEM((C, 2 * CELLS), BF),
            pltpu.VMEM((2, 3 * C, C), F32),
            pltpu.VMEM(cells, BF),
            pltpu.VMEM(cells, BF),
            pltpu.VMEM((2, CHIPS, deep, C), F32),
            pltpu.VMEM((2, CHIPS, deep, HALF), BF),
            pltpu.VMEM((2, CHIPS, deep, HALF), BF),
            pltpu.VMEM((2, CHIPS, deep, HALF), BF),
            pltpu.VMEM((2, CHIPS, deep, HALF), BF),
            pltpu.VMEM((ZS, 8, HALF), F32),
            pltpu.VMEM((ZS, 8, HALF), F32),
            pltpu.VMEM((8, HALF), F32),
            pltpu.VMEM((PLANE, 8, HALF), F32),
            pltpu.VMEM((6 * C // ZS, C), F32),
            pltpu.SemaphoreType.DMA((5,)),
            pltpu.SemaphoreType.DMA((10,)),
            pltpu.SemaphoreType.DMA((10,)),
            pltpu.SemaphoreType.DMA((4,)),
            pltpu.SemaphoreType.DMA((4,)),
            pltpu.SemaphoreType.DMA((12,)),
            pltpu.SemaphoreType.DMA((3,)),
            pltpu.SemaphoreType.REGULAR((3,)),
        ],
        compiler_params=pltpu.CompilerParams(
            collective_id=0, has_side_effects=True, vmem_limit_bytes=56 * 1024 * 1024
        ),
    )(
        segment_ids,
        clips.reshape(cells),
        spatial_weight.reshape(2, 3, 3, C, C),
        temporal_weight,
        upstream.reshape(cells),
    )
    grad, features, weight_grad = pl.pallas_call(
        finish,
        out_shape=outs,
        in_specs=[pl.BlockSpec(memory_space=pltpu.VMEM)] * 3,
        out_specs=(anywhere,) * 3,
        scratch_shapes=[pltpu.SemaphoreType.DMA((3,))],
    )(*parts)
    return (grad.reshape(clips.shape), features.reshape(clips.shape), weight_grad)


def solution(mesh):
    return jax.shard_map(
        local,
        mesh=mesh,
        in_specs=(
            P("dp", "tm", "rows", None, None),
            P("dp", None),
            P(),
            P(),
            P("dp", "tm", "rows", None, None),
        ),
        out_specs=(
            P("dp", "tm", "rows", None, None),
            P("dp", "tm", "rows", None, None),
            P("rows", None),
        ),
        check_vma=False,
    )
```

time: 67.4 us -> 59.1 us (0.88)
  local copies, waits for them, and re-layouts: 4.88 us -> 0 us
  Pallas kernels: 61.6 us -> 58.3 us
    unnamed x3 -> x0, local copies, waits for them, and re-layouts: 4.88 us -> none
    pallas_call x1 -> x2, Pallas kernels: 61.6 us -> 58.3 us  [the longest x1 56.4 us: local(): pl.pallas_call(kernel, out_shape=outs, in_specs=[pl.BlockSpec(memory_spac...]
where the time goes in v3:
time: 59.1 us; the launch traced here: 59 us
  Pallas kernels  58.3 us (99%)
  between operations  0.64 us (1%)
    pallas_call x1, Pallas kernels, local(): pl.pallas_call(kernel, out_shape=outs, in_specs=[pl.BlockSpec(memory_spac...  56.4 us
    pallas_call x1, Pallas kernels, local(): pl.pallas_call(finish, out_shape=outs, in_specs=[pl.BlockSpec(memory_spac...  1.89 us

profile of v3, /device:TPU:1, one launch (start us, length us, event | category | flops | bytes accessed | tf_op | source)
XLA Modules:
  0.0 59.0 jit_solution(13539318297061153204)
XLA Ops:
  0.6 56.4 %shard_map.76 = (bf16[2,4,64,256]{3,2,1,0:T(8,128)(2,1)}, bf16[2,4,64,256]{3,2,1,0:T(8,128)(2,1)}, f32[96,256]{1,0:T(8,128)}) custom-call(s32[1,16]{1,0:T(1,128)} %seg.1, bf16[2,4,64,256]{3,2,1,0:T(8,128)(2,1)} %bitcast.6, bf16[2,3,3,256,256]{4,3,2,1,0:T(8,128)(2,1)} %bitcast.5, bf16[2,3,256,256]{3,2,1,0:T(8,128)(2,1)} %time_w.1, bf16[2,4,64,256]{3,2,1,0:T(8,128)(2,1)} %bitcast.7), custom_call_target="tpu_custom_call" | custom-call | tf_op jit(solution)/shard_map/pallas_call | solution.py:462
  57.1 1.9 %shard_map.77 = (bf16[2,4,64,256]{3,2,1,0:T(8,128)(2,1)}, bf16[2,4,64,256]{3,2,1,0:T(8,128)(2,1)}, f32[96,256]{1,0:T(8,128)}) custom-call(bf16[2,4,64,256]{3,2,1,0:T(8,128)(2,1)} %get-tuple-element.9.grad_in, bf16[2,4,64,256]{3,2,1,0:T(8,128)(2,1)} %get-tuple-element.10.feat_in, f32[96,256]{1,0:T(8,128)} %get-tuple-element.11.weight_in), custom_call_target="tpu_custom_call" | custom-call | tf_op jit(solution)/shard_map/pallas_call | solution.py:514

commit v4 on v3

--- a/solution.py
+++ b/solution.py
@@ -19,15 +19,10 @@
 FRAMES = TS * OWN
 DEEP = ZS // 2
 BF, F32 = jnp.bfloat16, jnp.float32
-NT = (((1,), (1,)), ((), ()))
 
 
 def mm(left, right):
     return jnp.dot(left, right, preferred_element_type=F32)
-
-
-def mm_nt(left, right):
-    return lax.dot_general(left, right, NT, preferred_element_type=F32)
 
 
 def rows_of(padded, first, rows):
@@ -49,15 +44,18 @@
     return shifted(sums[0], 1) + sums[1] + shifted(sums[2], -1)
 
 
-def spatial_back(padded, weights):
+def spatial_back(padded, turned_weights):
     sums = []
     for kx in range(3):
-        total = None
-        for ky in range(3):
-            part = mm_nt(rows_of(padded, 2 - ky, ROWS), weights[ky, kx])
-            total = part if total is None else total + part
-        sums.append(total)
+        left = jnp.concatenate([rows_of(padded, 2 - ky, ROWS) for ky in range(3)], axis=1)
+        right = jnp.concatenate([turned_weights[ky, kx] for ky in range(3)], axis=0)
+        sums.append(mm(left, right))
     return shifted(sums[0], -1) + sums[1] + shifted(sums[2], 1)
+
+
+def far_first(rows, columns):
+    steps = [(i, j) for i in range(rows) for j in range(columns) if i or j]
+    return sorted(steps, key=lambda step: -min(step[0], rows - step[0]) - min(step[1], columns - step[1]))
 
 
 def finish(grad_in, feat_in, weight_in, grad_out, feat_out, weight_out, done):
@@ -70,11 +68,11 @@
 
 
 def kernel(
-    seg, clips, space_w, time_w, upstream,
+    segments, clips, space_w, time_w, upstream,
     grad_out, feat_out, weight_out,
-    ws, wt, x0, x1, act0, act1, slope0, slope1, g2, g1, dpre1, dpre0, dact, turned, part, feat, gin,
-    arranged, send_pair, recv_pair, send_plane, recv_plane, send_z, recv_z, total, recv_all, result,
-    load, wide_s, wide_r, near_s, near_r, sums, store, known,
+    ws, wt, wst, wtt, x0, x1, act0, act1, slope0, slope1, g2, g1, dpre1, dpre0, dact, turned, part,
+    arranged, send_pair, recv_pair, send_plane, recv_plane, send_z, recv_z, total, recv_all,
+    seg, load, wide_s, wide_r, near_s, near_r, sums, known,
 ):
     x = lax.axis_index("dp")
     t = lax.axis_index("tm")
@@ -86,12 +84,6 @@
     def at(dx, dt, dz):
         return {"dp": (x + dx) % XS, "tm": (t + dt) % TS, "rows": (z + dz) % ZS}
 
-    def plane_id(other):
-        return {"dp": other // TS, "tm": other % TS}
-
-    def chip_id(other):
-        return {"dp": other // YS, "tm": (other % YS) * CORES + core}
-
     near = [(0, dt, dz) for dt in (-1, 0, 1) for dz in (-1, 0, 1) if dt or dz]
     near += [(-1, 0, 0), (1, 0, 0), (0, -2, 0), (0, 2, 0)]
     second = [(0, 0, -2), (0, 0, 2), (-1, 0, 0), (1, 0, 0), (2, 0, 0)]
@@ -110,6 +102,7 @@
         pltpu.make_async_copy(time_w, wt, load.at[2]),
         pltpu.make_async_copy(upstream, g2.at[pl.ds(0, OWN), pl.ds(1, ROWS)], load.at[3]),
         pltpu.make_async_copy(space_w.at[1], ws.at[1], load.at[4]),
+        pltpu.make_async_copy(segments, seg, load.at[5]),
     ]
     for copy in loads:
         copy.start()
@@ -142,7 +135,7 @@
         blank(g2.at[pl.ds(OWN, OWN)])
         blank(g1.at[pl.ds(OWN, OWN)])
 
-    def remote(source, target, sems_s, sems_r, number, dt, dz):
+    def remote(source, target, sems_s, sems_r, number, dt, dz, only=None, edge=0):
         copy = pltpu.make_async_remote_copy(
             src_ref=source, dst_ref=target, send_sem=sems_s.at[number], recv_sem=sems_r.at[number],
             device_id=at(0, dt, dz),
@@ -160,6 +153,13 @@
         if dz == -1:
             sends.append(z > 0)
             takes.append(z < ZS - 1)
+        if edge:
+            inside = z > 0 if edge < 0 else z < ZS - 1
+            sends.append(inside)
+            takes.append(inside)
+        if only is not None:
+            sends.append(only)
+            takes.append(jnp.logical_not(only))
         send, take = sends[0], takes[0]
         for more in sends[1:]:
             send = send & more
@@ -188,8 +188,12 @@
     ]
     x_prior = [remote(clips, x0.at[prior, middle], wide_s, wide_r, 2, 1, 0)]
     x_corner = [
-        remote(x_high, x0.at[prior, top], wide_s, wide_r, 3, 1, 1),
-        remote(x_low, x0.at[prior, bottom], wide_s, wide_r, 4, 1, -1),
+        remote(x_high, x0.at[prior, top], wide_s, wide_r, 3, 1, 1, core == 1),
+        remote(x_low, x0.at[prior, bottom], wide_s, wide_r, 4, 1, -1, core == 1),
+    ]
+    x_handed = [
+        remote(x0.at[own, top], x0.at[prior, top], wide_s, wide_r, 10, 1, 0, core == 0, -1),
+        remote(x0.at[own, bottom], x0.at[prior, bottom], wide_s, wide_r, 11, 1, 0, core == 0, 1),
     ]
     g_low, g_high = upstream.at[:, pl.ds(0, 1)], upstream.at[:, pl.ds(ROWS - 1, 1)]
     now, after = pl.ds(0, OWN), pl.ds(OWN, OWN)
@@ -197,9 +201,15 @@
     g_halo = [
         remote(g_high, g2.at[now, over], wide_s, wide_r, 5, 0, 1),
         remote(g_low, g2.at[now, under], wide_s, wide_r, 6, 0, -1),
-        remote(upstream, g2.at[after, inner], wide_s, wide_r, 7, -1, 0),
-        remote(g_high, g2.at[after, over], wide_s, wide_r, 8, -1, 1),
-        remote(g_low, g2.at[after, under], wide_s, wide_r, 9, -1, -1),
+    ]
+    g_later = [remote(upstream, g2.at[after, inner], wide_s, wide_r, 7, -1, 0)]
+    g_corner = [
+        remote(g_high, g2.at[after, over], wide_s, wide_r, 8, -1, 1, core == 0),
+        remote(g_low, g2.at[after, under], wide_s, wide_r, 9, -1, -1, core == 0),
+    ]
+    g_handed = [
+        remote(g2.at[now, over], g2.at[after, over], wide_s, wide_r, 12, -1, 0, core == 1, -1),
+        remote(g2.at[now, under], g2.at[after, under], wide_s, wide_r, 13, -1, 0, core == 1, 1),
     ]
     act_copy = [remote(act1.at[own], act1.at[prior], near_s, near_r, 0, 1, 0)]
     g1_copy = [remote(g1.at[now], g1.at[after], near_s, near_r, 1, -1, 0)]
@@ -208,17 +218,8 @@
         remote(dpre0.at[:, pl.ds(1, 1)], dpre0.at[:, under], near_s, near_r, 3, 0, -1),
     ]
 
-    def one_clip(frame, offset):
-        before = jnp.maximum(frame - offset, 0)
-        same = (frame - offset >= 0) & (frame < FRAMES) & (seg[0, before] == seg[0, jnp.minimum(frame, FRAMES - 1)])
-        return jnp.where(same, 1.0, 0.0)
-
-    first_frame = t * OWN
-    back_mask = [[one_clip(first_frame + i, k) for i in range(OWN)] for k in range(3)]
-    next_mask = [[one_clip(first_frame + i + k, k) for i in range(OWN)] for k in range(3)]
-
     def gated(values, mask):
-        return (values.astype(F32) * mask).astype(BF)
+        return values * mask.astype(BF)
 
     def temporal(base, acts, weights):
         rows = base.shape[1]
@@ -237,11 +238,9 @@
             frames = [gated(frames[i], next_mask[k][i]) for i in range(OWN)]
         return jnp.stack(frames).reshape(OWN * frames[0].shape[0] * COLS, C)
 
-    def grad_of_act(grads, weights):
-        out = mm_nt(lifted(grads, 0), weights[0])
-        for k in range(1, 3):
-            out = out + mm_nt(lifted(grads, k), weights[k])
-        return out
+    def grad_of_act(grads, turned_weights):
+        left = jnp.concatenate([lifted(grads, k) for k in range(3)], axis=1)
+        return mm(left, turned_weights.reshape(3 * C, C))
 
     def slope(pre, sigma):
         return sigma * (1.0 + pre * (1.0 - sigma))
@@ -250,12 +249,32 @@
     start(x_halo)
     start(x_prior)
     start(x_corner)
+    start(g_later)
     tell(known.at[0], near)
 
-    loads[0].wait()
-    loads[1].wait()
+    for copy in loads:
+        copy.wait()
+
+    def one_clip(frame, offset):
+        before = jnp.maximum(frame - offset, 0)
+        same = (frame - offset >= 0) & (frame < FRAMES) & (seg[0, before] == seg[0, jnp.minimum(frame, FRAMES - 1)])
+        return jnp.where(same, 1.0, 0.0)
+
+    first_frame = t * OWN
+    back_mask = [[one_clip(first_frame + i, k) for i in range(OWN)] for k in range(3)]
+    next_mask = [[one_clip(first_frame + i + k, k) for i in range(OWN)] for k in range(3)]
+
+    @pl.loop(0, 3)
+    def _(index):
+        for layer in range(2):
+            for kx in range(3):
+                wst[layer, index, kx] = ws[layer, index, kx].T
+            wtt[layer, index] = wt[layer, index].T
+
     arrived(x_halo)
+    start(x_handed)
     start(g_halo)
+    start(g_corner)
     wide = (OWN, ROWS + 4, COLS, C)
     pre = spatial(x0.at[own], ws.at[0], ROWS + 4)
     sigma = jax.nn.sigmoid(pre)
@@ -269,13 +288,13 @@
 
     for i in range(OWN):
         turn(OWN + i)
-    loads[2].wait()
-    loads[3].wait()
-    loads[4].wait()
     arrived(x_prior)
     arrived(x_corner)
+    arrived(x_handed)
     pre = spatial(x0.at[prior], ws.at[0], ROWS + 4)
     act0[:OWN] = (pre * jax.nn.sigmoid(pre)).astype(BF).reshape(wide)
+    arrived(g_halo)
+    start(g_handed)
     x1[...] = temporal(x0[OWN:, 1 : ROWS + 5], act0, wt[0])
 
     @pl.when(first)
@@ -292,8 +311,10 @@
     act1[OWN:] = (pre * sigma).astype(BF).reshape(tall)[:, 1 : ROWS + 1]
     slope1[...] = slope(pre, sigma)
     start(act_copy)
-    arrived(g_halo)
-    dact[...] = grad_of_act(g2, wt[1])
+    arrived(g_later)
+    arrived(g_corner)
+    arrived(g_handed)
+    dact[...] = grad_of_act(g2, wtt[1])
     dpre1[...] = (dact[...] * slope1[...]).astype(BF).reshape(tall)
 
     @pl.when(first)
@@ -305,7 +326,7 @@
         blank(dpre1.at[:, under])
 
     g1[:OWN] = (
-        g2[:OWN, 1 : ROWS + 1].astype(F32) + spatial_back(dpre1, ws.at[1]).reshape(OWN, ROWS, COLS, C)
+        g2[:OWN, 1 : ROWS + 1].astype(F32) + spatial_back(dpre1, wst.at[1]).reshape(OWN, ROWS, COLS, C)
     ).astype(BF)
     start(g1_copy)
     for i in range(OWN):
@@ -350,12 +371,12 @@
             mine = jnp.where(core == 0, rows[:, :HALF], rows[:, HALF:])
             send_plane[layer, group] = (mine + recv_pair[layer, group].astype(F32)).astype(BF)
 
-        @pl.loop(1, CHIPS)
-        def _(step):
-            other = (chip + step) % CHIPS
+        for dx, dy in far_first(XS, YS):
+            target = at(dx, CORES * dy, 0)
+            other = target["dp"] * YS + target["tm"] // CORES
             pltpu.make_async_remote_copy(
                 src_ref=send_plane.at[layer, other], dst_ref=recv_plane.at[layer, chip],
-                send_sem=sums.at[4 + layer], recv_sem=sums.at[6 + layer], device_id=chip_id(other),
+                send_sem=sums.at[4 + layer], recv_sem=sums.at[6 + layer], device_id=target,
             ).start()
 
         recv_plane[layer, chip] = send_plane[layer, chip]
@@ -363,7 +384,7 @@
     def gather(layer):
         pltpu.make_async_remote_copy(
             src_ref=send_plane.at[layer, pl.ds(0, CHIPS - 1)], dst_ref=recv_plane.at[layer, pl.ds(0, CHIPS - 1)],
-            send_sem=sums.at[4 + layer], recv_sem=sums.at[6 + layer], device_id=chip_id((chip + 1) % CHIPS),
+            send_sem=sums.at[4 + layer], recv_sem=sums.at[6 + layer], device_id=at(1, 0, 0),
         ).wait()
         summed = recv_plane[layer, 0].astype(F32)
         for group in range(1, CHIPS):
@@ -384,36 +405,30 @@
                 ).start()
 
     arrange(0)
+    pl.semaphore_wait(known.at[1], len(second))
+    tell(known.at[2], third)
     turned_own = act1[OWN:].reshape(CELLS, C).T
     for k in range(3):
         frames = [g2[i + k, 1 : ROWS + 1] for i in range(OWN)]
         if k:
             frames = [gated(frames[i], next_mask[k][i]) for i in range(OWN)]
         part[1, k * C : (k + 1) * C] = mm(turned_own, jnp.stack(frames).reshape(CELLS, C))
+    spread(0)
     arrange(1)
-    pl.semaphore_wait(known.at[1], len(second))
-    tell(known.at[2], third)
-    spread(0)
-    spread(1)
-
     arrived(g1_copy)
-    dpre0[:, 1 : ROWS + 1] = (grad_of_act(g1, wt[0]) * slope0[...]).astype(BF).reshape(OWN, ROWS, COLS, C)
+    dpre0[:, 1 : ROWS + 1] = (grad_of_act(g1, wtt[0]) * slope0[...]).astype(BF).reshape(OWN, ROWS, COLS, C)
     start(d_halo)
     pl.semaphore_wait(known.at[2], len(third))
     gather(0)
+    spread(1)
+    arrived(act_copy)
+    feat_out[...] = temporal(x1[:, 2 : ROWS + 2], act1, wt[1])
     gather(1)
     recv_z[z] = send_z[z]
-
-    arrived(act_copy)
-    feat[...] = temporal(x1[:, 2 : ROWS + 2], act1, wt[1])
-    feat_store = pltpu.make_async_copy(feat, feat_out, store.at[0])
-    feat_store.start()
     arrived(d_halo)
-    gin[...] = (
-        g1[:OWN].astype(F32) + spatial_back(dpre0, ws.at[0]).reshape(OWN, ROWS, COLS, C)
+    grad_out[...] = (
+        g1[:OWN].astype(F32) + spatial_back(dpre0, wst.at[0]).reshape(OWN, ROWS, COLS, C)
     ).astype(BF)
-    gin_store = pltpu.make_async_copy(gin, grad_out, store.at[1])
-    gin_store.start()
 
     pltpu.make_async_remote_copy(
         src_ref=send_z.at[pl.ds(0, ZS - 1)], dst_ref=recv_z.at[pl.ds(0, ZS - 1)],
@@ -424,30 +439,24 @@
         final = final + recv_z[block]
     total[...] = final
 
-    @pl.loop(1, PLANE)
-    def _(step):
+    for dx, dt in far_first(XS, TS):
         pltpu.make_async_remote_copy(
             src_ref=total, dst_ref=recv_all.at[place], send_sem=sums.at[10], recv_sem=sums.at[11],
-            device_id=plane_id((place + step) % PLANE),
+            device_id=at(dx, dt, 0),
         ).start()
 
     recv_all[place] = final
-    for group in (x_halo, x_prior, x_corner, g_halo, act_copy, g1_copy, d_halo):
+    for group in (x_halo, x_prior, x_corner, x_handed, g_halo, g_later, g_corner, g_handed, act_copy, g1_copy, d_halo):
         sent(group)
-    feat_store.wait()
-    gin_store.wait()
     pltpu.make_async_remote_copy(
         src_ref=recv_all.at[pl.ds(0, PLANE - 1)], dst_ref=recv_all.at[pl.ds(0, PLANE - 1)],
-        send_sem=sums.at[10], recv_sem=sums.at[11], device_id=plane_id((place + 1) % PLANE),
+        send_sem=sums.at[10], recv_sem=sums.at[11], device_id=at(1, 0, 0),
     ).wait()
     for group in range(CHIPS):
         for half in range(CORES):
-            result[PIECE * group : PIECE * (group + 1), HALF * half : HALF * (half + 1)] = recv_all[
+            weight_out[PIECE * group : PIECE * (group + 1), HALF * half : HALF * (half + 1)] = recv_all[
                 group * CORES + half, :PIECE, :
             ]
-    weight_store = pltpu.make_async_copy(result, weight_out, store.at[2])
-    weight_store.start()
-    weight_store.wait()
 
 
 def local(clips, segment_ids, spatial_weight, temporal_weight, upstream):
@@ -459,12 +468,16 @@
         jax.ShapeDtypeStruct(cells, BF),
         jax.ShapeDtypeStruct((6 * C // ZS, C), F32),
     )
+    kept = tuple(pltpu.VMEM(out.shape, out.dtype) for out in outs)
+    inside = pl.BlockSpec(memory_space=pltpu.VMEM)
     parts = pl.pallas_call(
         kernel,
-        out_shape=outs,
-        in_specs=[pl.BlockSpec(memory_space=pltpu.SMEM)] + [anywhere] * 4,
-        out_specs=(anywhere,) * 3,
+        out_shape=kept,
+        in_specs=[anywhere] * 5,
+        out_specs=(inside,) * 3,
         scratch_shapes=[
+            pltpu.VMEM((2, 3, 3, C, C), BF),
+            pltpu.VMEM((2, 3, C, C), BF),
             pltpu.VMEM((2, 3, 3, C, C), BF),
             pltpu.VMEM((2, 3, C, C), BF),
             pltpu.VMEM((2 * OWN, ROWS + 6, COLS, C), BF),
@@ -480,8 +493,6 @@
             pltpu.VMEM((OWN * (ROWS + 2) * COLS, C), F32),
             pltpu.VMEM((C, 2 * CELLS), BF),
             pltpu.VMEM((2, 3 * C, C), F32),
-            pltpu.VMEM(cells, BF),
-            pltpu.VMEM(cells, BF),
             pltpu.VMEM((2, CHIPS, deep, C), F32),
             pltpu.VMEM((2, CHIPS, deep, HALF), BF),
             pltpu.VMEM((2, CHIPS, deep, HALF), BF),
@@ -491,14 +502,13 @@
             pltpu.VMEM((ZS, 8, HALF), F32),
             pltpu.VMEM((8, HALF), F32),
             pltpu.VMEM((PLANE, 8, HALF), F32),
-            pltpu.VMEM((6 * C // ZS, C), F32),
-            pltpu.SemaphoreType.DMA((5,)),
-            pltpu.SemaphoreType.DMA((10,)),
-            pltpu.SemaphoreType.DMA((10,)),
+            pltpu.SMEM((1, FRAMES), jnp.int32),
+            pltpu.SemaphoreType.DMA((6,)),
+            pltpu.SemaphoreType.DMA((14,)),
+            pltpu.SemaphoreType.DMA((14,)),
             pltpu.SemaphoreType.DMA((4,)),
             pltpu.SemaphoreType.DMA((4,)),
             pltpu.SemaphoreType.DMA((12,)),
-            pltpu.SemaphoreType.DMA((3,)),
             pltpu.SemaphoreType.REGULAR((3,)),
         ],
         compiler_params=pltpu.CompilerParams(
@@ -511,10 +521,11 @@
         temporal_weight,
         upstream.reshape(cells),
     )
+    parts = [pltpu.with_memory_space_constraint(part, pltpu.VMEM) for part in parts]
     grad, features, weight_grad = pl.pallas_call(
         finish,
         out_shape=outs,
-        in_specs=[pl.BlockSpec(memory_space=pltpu.VMEM)] * 3,
+        in_specs=[inside] * 3,
         out_specs=(anywhere,) * 3,
         scratch_shapes=[pltpu.SemaphoreType.DMA((3,))],
     )(*parts)

time: 59.1 us -> 52.9 us (0.90)
  Pallas kernels: 58.3 us -> 52.2 us
    pallas_call x2, Pallas kernels: 58.3 us -> 52.2 us  [the longest x1 51.3 us: local(): pl.pallas_call(kernel, out_shape=kept, in_specs=[anywhere] * 5, out_specs...]
where the time goes in v4:
time: 52.9 us; the launch traced here: 52.8 us
  Pallas kernels  52.2 us (99%)
  between operations  0.64 us (1%)
    pallas_call x1, Pallas kernels, local(): pl.pallas_call(kernel, out_shape=kept, in_specs=[anywhere] * 5, out_specs...  51.3 us

profile of v4, /device:TPU:1, one launch (start us, length us, event | category | flops | bytes accessed | tf_op | source)
XLA Modules:
  0.0 52.8 jit_solution(11365041511605766034)
XLA Ops:
  0.6 51.3 %shard_map.76 = (bf16[2,4,64,256]{3,2,1,0:T(8,128)(2,1)S(1)}, bf16[2,4,64,256]{3,2,1,0:T(8,128)(2,1)S(1)}, f32[96,256]{1,0:T(8,128)S(1)}) custom-call(s32[1,16]{1,0:T(1,128)} %segments.1, bf16[2,4,64,256]{3,2,1,0:T(8,128)(2,1)} %bitcast.6, bf16[2,3,3,256,256]{4,3,2,1,0:T(8,128)(2,1)} %bitcast.5, bf16[2,3,256,256]{3,2,1,0:T(8,128)(2,1)} %time_w.1, ...), custom_call_target="tpu_custom_call" | custom-call | tf_op jit(solution)/shard_map/pallas_call | solution.py:473
  52.0 0.8 %shard_map.77 = (bf16[2,4,64,256]{3,2,1,0:T(8,128)(2,1)}, bf16[2,4,64,256]{3,2,1,0:T(8,128)(2,1)}, f32[96,256]{1,0:T(8,128)}) custom-call(bf16[2,4,64,256]{3,2,1,0:T(8,128)(2,1)S(1)} %get-tuple-element.9.grad_in, bf16[2,4,64,256]{3,2,1,0:T(8,128)(2,1)S(1)} %get-tuple-element.10.feat_in, f32[96,256]{1,0:T(8,128)S(1)} %get-tuple-element.11.weight_in), custom_call_target="tpu_custom_call" | custom-call | tf_op jit(solution)/shard_map/pallas_call | solution.py:525

commit v5 on v4

--- a/solution.py
+++ b/solution.py
@@ -26,7 +26,7 @@
 
 
 def rows_of(padded, first, rows):
-    return padded[:, first : first + rows].reshape(OWN * rows * COLS, C)
+    return padded[first : first + rows].reshape(rows * COLS, C)
 
 
 def shifted(values, by):
@@ -221,25 +221,24 @@
     def gated(values, mask):
         return values * mask.astype(BF)
 
-    def temporal(base, acts, weights):
-        rows = base.shape[1]
+    def temporal(base, acts, weights, i):
         columns = []
         for k in range(3):
-            frames = [acts[OWN + i - k] for i in range(OWN)]
+            frame = acts[OWN + i - k]
             if k:
-                frames = [gated(frames[i], back_mask[k][i]) for i in range(OWN)]
-            columns.append(jnp.stack(frames).reshape(OWN * rows * COLS, C))
+                frame = gated(frame, back_mask(k, i))
+            columns.append(frame.reshape(base.shape[0] * COLS, C))
         out = mm(jnp.concatenate(columns, axis=1), weights.reshape(3 * C, C))
         return (base.astype(F32) + out.reshape(base.shape)).astype(BF)
 
-    def lifted(grads, k):
-        frames = [grads[i + k] for i in range(OWN)]
+    def lifted(grads, k, rows):
+        frames = [grads[i + k, rows] for i in range(OWN)]
         if k:
-            frames = [gated(frames[i], next_mask[k][i]) for i in range(OWN)]
+            frames = [gated(frames[i], next_mask(k, i)) for i in range(OWN)]
         return jnp.stack(frames).reshape(OWN * frames[0].shape[0] * COLS, C)
 
-    def grad_of_act(grads, turned_weights):
-        left = jnp.concatenate([lifted(grads, k) for k in range(3)], axis=1)
+    def grad_of_act(grads, turned_weights, rows):
+        left = jnp.concatenate([lifted(grads, k, rows) for k in range(3)], axis=1)
         return mm(left, turned_weights.reshape(3 * C, C))
 
     def slope(pre, sigma):
@@ -261,8 +260,12 @@
         return jnp.where(same, 1.0, 0.0)
 
     first_frame = t * OWN
-    back_mask = [[one_clip(first_frame + i, k) for i in range(OWN)] for k in range(3)]
-    next_mask = [[one_clip(first_frame + i + k, k) for i in range(OWN)] for k in range(3)]
+
+    def back_mask(k, i):
+        return one_clip(first_frame + i, k)
+
+    def next_mask(k, i):
+        return one_clip(first_frame + i + k, k)
 
     @pl.loop(0, 3)
     def _(index):
@@ -275,27 +278,38 @@
     start(x_handed)
     start(g_halo)
     start(g_corner)
-    wide = (OWN, ROWS + 4, COLS, C)
-    pre = spatial(x0.at[own], ws.at[0], ROWS + 4)
-    sigma = jax.nn.sigmoid(pre)
-    act0[OWN:] = (pre * sigma).astype(BF).reshape(wide)
-    slope0[...] = slope(pre, sigma).reshape(wide)[:, 2 : ROWS + 2].reshape(CELLS, C)
-    pl.semaphore_wait(known.at[0], len(near))
-    tell(known.at[1], second)
-
-    def turn(i):
-        turned[:, i * 256 : (i + 1) * 256] = act0[i, 2 : ROWS + 2].reshape(256, C).T
-
-    for i in range(OWN):
-        turn(OWN + i)
-    arrived(x_prior)
-    arrived(x_corner)
-    arrived(x_handed)
-    pre = spatial(x0.at[prior], ws.at[0], ROWS + 4)
-    act0[:OWN] = (pre * jax.nn.sigmoid(pre)).astype(BF).reshape(wide)
+    wide, tall, flat = (ROWS + 4, COLS, C), (ROWS + 2, COLS, C), (ROWS, COLS, C)
+
+    @pl.loop(0, 2 * OWN)
+    def _(step):
+        frame = (step + OWN) % (2 * OWN)
+
+        @pl.when(step == OWN)
+        def _():
+            pl.semaphore_wait(known.at[0], len(near))
+            tell(known.at[1], second)
+            arrived(g_later)
+            dact[:, inner] = grad_of_act(g2, wtt[1], inner).reshape(OWN, ROWS, COLS, C)
+            arrived(x_prior)
+            arrived(x_corner)
+            arrived(x_handed)
+
+        pre = spatial(x0.at[frame], ws.at[0], ROWS + 4)
+        sigma = jax.nn.sigmoid(pre)
+        act = (pre * sigma).astype(BF).reshape(wide)
+        act0[frame] = act
+        turned[:, pl.ds(pl.multiple_of(frame * 256, 256), 256)] = act[2 : ROWS + 2].reshape(256, C).T
+
+        @pl.when(step < OWN)
+        def _():
+            slope0[step] = slope(pre, sigma).reshape(wide)[2 : ROWS + 2]
+
     arrived(g_halo)
     start(g_handed)
-    x1[...] = temporal(x0[OWN:, 1 : ROWS + 5], act0, wt[0])
+
+    @pl.loop(0, OWN)
+    def _(i):
+        x1[i] = temporal(x0[OWN + i, 1 : ROWS + 5], act0, wt[0], i)
 
     @pl.when(first)
     def _():
@@ -305,17 +319,19 @@
     def _():
         blank(x1.at[:, pl.ds(ROWS + 2, 2)])
 
-    tall = (OWN, ROWS + 2, COLS, C)
-    pre = spatial(x1, ws.at[1], ROWS + 2)
-    sigma = jax.nn.sigmoid(pre)
-    act1[OWN:] = (pre * sigma).astype(BF).reshape(tall)[:, 1 : ROWS + 1]
-    slope1[...] = slope(pre, sigma)
+    @pl.loop(0, OWN)
+    def _(i):
+        pre = spatial(x1.at[i], ws.at[1], ROWS + 2)
+        sigma = jax.nn.sigmoid(pre)
+        act1[OWN + i] = (pre * sigma).astype(BF).reshape(tall)[1 : ROWS + 1]
+        slope1[i] = slope(pre, sigma).reshape(tall)
+
     start(act_copy)
-    arrived(g_later)
     arrived(g_corner)
     arrived(g_handed)
-    dact[...] = grad_of_act(g2, wtt[1])
-    dpre1[...] = (dact[...] * slope1[...]).astype(BF).reshape(tall)
+    for edge in (over, under):
+        dact[:, edge] = grad_of_act(g2, wtt[1], edge).reshape(OWN, 1, COLS, C)
+    dpre1[...] = (dact[...] * slope1[...]).astype(BF)
 
     @pl.when(first)
     def _():
@@ -325,16 +341,16 @@
     def _():
         blank(dpre1.at[:, under])
 
-    g1[:OWN] = (
-        g2[:OWN, 1 : ROWS + 1].astype(F32) + spatial_back(dpre1, wst.at[1]).reshape(OWN, ROWS, COLS, C)
-    ).astype(BF)
+    @pl.loop(0, OWN)
+    def _(i):
+        back = spatial_back(dpre1.at[i], wst.at[1]).reshape(flat)
+        g1[i] = (g2[i, 1 : ROWS + 1].astype(F32) + back).astype(BF)
+
     start(g1_copy)
-    for i in range(OWN):
-        turn(i)
     for k in range(3):
         frames = [g1[i] for i in range(OWN)]
         if k:
-            frames = [gated(frames[i], back_mask[k][i]) for i in range(OWN)]
+            frames = [gated(frames[i], back_mask(k, i)) for i in range(OWN)]
         part[0, k * C : (k + 1) * C] = mm(
             turned[:, (OWN - k) * 256 : (2 * OWN - k) * 256], jnp.stack(frames).reshape(CELLS, C)
         )
@@ -411,24 +427,29 @@
     for k in range(3):
         frames = [g2[i + k, 1 : ROWS + 1] for i in range(OWN)]
         if k:
-            frames = [gated(frames[i], next_mask[k][i]) for i in range(OWN)]
+            frames = [gated(frames[i], next_mask(k, i)) for i in range(OWN)]
         part[1, k * C : (k + 1) * C] = mm(turned_own, jnp.stack(frames).reshape(CELLS, C))
     spread(0)
     arrange(1)
     arrived(g1_copy)
-    dpre0[:, 1 : ROWS + 1] = (grad_of_act(g1, wtt[0]) * slope0[...]).astype(BF).reshape(OWN, ROWS, COLS, C)
+    dpre0[:, 1 : ROWS + 1] = (grad_of_act(g1, wtt[0], pl.ds(0, ROWS)) * slope0[...].reshape(CELLS, C)).astype(BF).reshape(OWN, ROWS, COLS, C)
     start(d_halo)
     pl.semaphore_wait(known.at[2], len(third))
     gather(0)
     spread(1)
     arrived(act_copy)
-    feat_out[...] = temporal(x1[:, 2 : ROWS + 2], act1, wt[1])
+
+    @pl.loop(0, OWN)
+    def _(i):
+        feat_out[i] = temporal(x1[i, 2 : ROWS + 2], act1, wt[1], i)
+
     gather(1)
     recv_z[z] = send_z[z]
     arrived(d_halo)
-    grad_out[...] = (
-        g1[:OWN].astype(F32) + spatial_back(dpre0, wst.at[0]).reshape(OWN, ROWS, COLS, C)
-    ).astype(BF)
+
+    @pl.loop(0, OWN)
+    def _(i):
+        grad_out[i] = (g1[i].astype(F32) + spatial_back(dpre0.at[i], wst.at[0]).reshape(flat)).astype(BF)
 
     pltpu.make_async_remote_copy(
         src_ref=send_z.at[pl.ds(0, ZS - 1)], dst_ref=recv_z.at[pl.ds(0, ZS - 1)],
@@ -484,13 +505,13 @@
             pltpu.VMEM((OWN, ROWS + 4, COLS, C), BF),
             pltpu.VMEM((2 * OWN, ROWS + 4, COLS, C), BF),
             pltpu.VMEM((2 * OWN, ROWS, COLS, C), BF),
-            pltpu.VMEM((CELLS, C), F32),
-            pltpu.VMEM((OWN * (ROWS + 2) * COLS, C), F32),
+            pltpu.VMEM((OWN, ROWS, COLS, C), F32),
+            pltpu.VMEM((OWN, ROWS + 2, COLS, C), F32),
             pltpu.VMEM((2 * OWN, ROWS + 2, COLS, C), BF),
             pltpu.VMEM((2 * OWN, ROWS, COLS, C), BF),
             pltpu.VMEM((OWN, ROWS + 2, COLS, C), BF),
             pltpu.VMEM((OWN, ROWS + 2, COLS, C), BF),
-            pltpu.VMEM((OWN * (ROWS + 2) * COLS, C), F32),
+            pltpu.VMEM((OWN, ROWS + 2, COLS, C), F32),
             pltpu.VMEM((C, 2 * CELLS), BF),
             pltpu.VMEM((2, 3 * C, C), F32),
             pltpu.VMEM((2, CHIPS, deep, C), F32),

time: 52.9 us -> 52.1 us (0.985)
  Pallas kernels: 52.2 us -> 51.3 us
    pallas_call x1, Pallas kernels: 51.3 us -> 50.5 us  [local(): pl.pallas_call(kernel, out_shape=kept, in_specs=[anywhere] * 5, out_specs...]
where the time goes in v5:
time: 52.1 us; the launch traced here: 52 us
  Pallas kernels  51.3 us (98%)
  between operations  0.64 us (1%)
    pallas_call x1, Pallas kernels, local(): pl.pallas_call(kernel, out_shape=kept, in_specs=[anywhere] * 5, out_specs...  50.5 us

profile of v5, /device:TPU:1, one launch (start us, length us, event | category | flops | bytes accessed | tf_op | source)
XLA Modules:
  0.0 52.0 jit_solution(8358854008416793171)
XLA Ops:
  0.6 50.5 %shard_map.76 = (bf16[2,4,64,256]{3,2,1,0:T(8,128)(2,1)S(1)}, bf16[2,4,64,256]{3,2,1,0:T(8,128)(2,1)S(1)}, f32[96,256]{1,0:T(8,128)S(1)}) custom-call(s32[1,16]{1,0:T(1,128)} %segments.1, bf16[2,4,64,256]{3,2,1,0:T(8,128)(2,1)} %bitcast.6, bf16[2,3,3,256,256]{4,3,2,1,0:T(8,128)(2,1)} %bitcast.5, bf16[2,3,256,256]{3,2,1,0:T(8,128)(2,1)} %time_w.1, ...), custom_call_target="tpu_custom_call" | custom-call | tf_op jit(solution)/shard_map/pallas_call | solution.py:494
  51.1 0.8 %shard_map.77 = (bf16[2,4,64,256]{3,2,1,0:T(8,128)(2,1)}, bf16[2,4,64,256]{3,2,1,0:T(8,128)(2,1)}, f32[96,256]{1,0:T(8,128)}) custom-call(bf16[2,4,64,256]{3,2,1,0:T(8,128)(2,1)S(1)} %get-tuple-element.9.grad_in, bf16[2,4,64,256]{3,2,1,0:T(8,128)(2,1)S(1)} %get-tuple-element.10.feat_in, f32[96,256]{1,0:T(8,128)S(1)} %get-tuple-element.11.weight_in), custom_call_target="tpu_custom_call" | custom-call | tf_op jit(solution)/shard_map/pallas_call | solution.py:546

commit v6 on v5

--- a/solution.py
+++ b/solution.py
@@ -245,9 +245,9 @@
         return sigma * (1.0 + pre * (1.0 - sigma))
 
     pl.semaphore_wait(barrier, len(near))
-    start(x_halo)
+    pl.when(core == 0)(lambda: start(x_halo))
+    start(x_corner)
     start(x_prior)
-    start(x_corner)
     start(g_later)
     tell(known.at[0], near)
 
@@ -273,6 +273,8 @@
             for kx in range(3):
                 wst[layer, index, kx] = ws[layer, index, kx].T
             wtt[layer, index] = wt[layer, index].T
+
+    pl.when(core == 1)(lambda: start(x_halo))
 
     arrived(x_halo)
     start(x_handed)

time: 52.1 us -> 51.2 us (0.983)
  Pallas kernels: 51.3 us -> 50.4 us
    pallas_call x1, Pallas kernels: 50.5 us -> 49.6 us  [local(): pl.pallas_call(kernel, out_shape=kept, in_specs=[anywhere] * 5, out_specs...]
where the time goes in v6:
time: 51.2 us; the launch traced here: 51 us
  Pallas kernels  50.4 us (98%)
  between operations  0.64 us (1%)
    pallas_call x1, Pallas kernels, local(): pl.pallas_call(kernel, out_shape=kept, in_specs=[anywhere] * 5, out_specs...  49.6 us

profile of v6, /device:TPU:1, one launch (start us, length us, event | category | flops | bytes accessed | tf_op | source)
XLA Modules:
  0.0 51.0 jit_solution(4252256855855306370)
XLA Ops:
  0.6 49.6 %shard_map.76 = (bf16[2,4,64,256]{3,2,1,0:T(8,128)(2,1)S(1)}, bf16[2,4,64,256]{3,2,1,0:T(8,128)(2,1)S(1)}, f32[96,256]{1,0:T(8,128)S(1)}) custom-call(s32[1,16]{1,0:T(1,128)} %segments.1, bf16[2,4,64,256]{3,2,1,0:T(8,128)(2,1)} %bitcast.6, bf16[2,3,3,256,256]{4,3,2,1,0:T(8,128)(2,1)} %bitcast.5, bf16[2,3,256,256]{3,2,1,0:T(8,128)(2,1)} %time_w.1, ...), custom_call_target="tpu_custom_call" | custom-call | tf_op jit(solution)/shard_map/pallas_call | solution.py:496
  50.2 0.8 %shard_map.77 = (bf16[2,4,64,256]{3,2,1,0:T(8,128)(2,1)}, bf16[2,4,64,256]{3,2,1,0:T(8,128)(2,1)}, f32[96,256]{1,0:T(8,128)}) custom-call(bf16[2,4,64,256]{3,2,1,0:T(8,128)(2,1)S(1)} %get-tuple-element.9.grad_in, bf16[2,4,64,256]{3,2,1,0:T(8,128)(2,1)S(1)} %get-tuple-element.10.feat_in, f32[96,256]{1,0:T(8,128)S(1)} %get-tuple-element.11.weight_in), custom_call_target="tpu_custom_call" | custom-call | tf_op jit(solution)/shard_map/pallas_call | solution.py:548

commit v7 on v6

--- a/solution.py
+++ b/solution.py
@@ -375,8 +375,8 @@
 
         @pl.loop(0, CHIPS)
         def _(group):
-            rows = arranged[layer, group]
-            send_pair[layer, group] = jnp.where(core == 0, rows[:, HALF:], rows[:, :HALF]).astype(BF)
+            other = pl.ds(pl.multiple_of((1 - core) * HALF, HALF), HALF)
+            send_pair[layer, group] = arranged[layer, group, :, other].astype(BF)
 
         pair_copy(layer).start()
 
@@ -385,8 +385,7 @@
 
         @pl.loop(0, CHIPS)
         def _(group):
-            rows = arranged[layer, group]
-            mine = jnp.where(core == 0, rows[:, :HALF], rows[:, HALF:])
+            mine = arranged[layer, group, :, pl.ds(pl.multiple_of(core * HALF, HALF), HALF)]
             send_plane[layer, group] = (mine + recv_pair[layer, group].astype(F32)).astype(BF)
 
         for dx, dy in far_first(XS, YS):

time: 51.2 us -> 51.2 us (level)
  no operation moved by 1% of the time
where the time goes in v7:
time: 51.2 us; the launch traced here: 51.1 us
  Pallas kernels  50.4 us (98%)
  between operations  0.64 us (1%)
    pallas_call x1, Pallas kernels, local(): pl.pallas_call(kernel, out_shape=kept, in_specs=[anywhere] * 5, out_specs...  49.6 us

profile of v7, /device:TPU:1, one launch (start us, length us, event | category | flops | bytes accessed | tf_op | source)
XLA Modules:
  0.0 51.1 jit_solution(11257002787139674133)
XLA Ops:
  0.6 49.6 %shard_map.76 = (bf16[2,4,64,256]{3,2,1,0:T(8,128)(2,1)S(1)}, bf16[2,4,64,256]{3,2,1,0:T(8,128)(2,1)S(1)}, f32[96,256]{1,0:T(8,128)S(1)}) custom-call(s32[1,16]{1,0:T(1,128)} %segments.1, bf16[2,4,64,256]{3,2,1,0:T(8,128)(2,1)} %bitcast.6, bf16[2,3,3,256,256]{4,3,2,1,0:T(8,128)(2,1)} %bitcast.5, bf16[2,3,256,256]{3,2,1,0:T(8,128)(2,1)} %time_w.1, ...), custom_call_target="tpu_custom_call" | custom-call | tf_op jit(solution)/shard_map/pallas_call | solution.py:495
  50.2 0.8 %shard_map.77 = (bf16[2,4,64,256]{3,2,1,0:T(8,128)(2,1)}, bf16[2,4,64,256]{3,2,1,0:T(8,128)(2,1)}, f32[96,256]{1,0:T(8,128)}) custom-call(bf16[2,4,64,256]{3,2,1,0:T(8,128)(2,1)S(1)} %get-tuple-element.9.grad_in, bf16[2,4,64,256]{3,2,1,0:T(8,128)(2,1)S(1)} %get-tuple-element.10.feat_in, f32[96,256]{1,0:T(8,128)S(1)} %get-tuple-element.11.weight_in), custom_call_target="tpu_custom_call" | custom-call | tf_op jit(solution)/shard_map/pallas_call | solution.py:547
